TPU v7x, 512 devices: a whole 4x8x8 slice. The times are simulated.
512 devices in a mesh: span: 64 (over x, z, core), wall: 8 (over y).
Axes of the slice: x: 4, y: 8, z: 8, core: 2. Of those that a mesh axis runs over, the one named last changes fastest.
Arguments:
- velocity: float32 [3, 2, 1536, 8192], P(None, None, 'wall', 'span'), may hold values from -6 to 6
- wave_x: float32 [2], replicated, may hold values from 0.01 to 0.1
Outputs:
- pressure: float32 [2, 1536, 8192], P(None, 'wall', 'span')
All inputs are finite; a program needn't handle non-finite values.
Results may differ from a plain program's by a relative error of at most 0.0023.
Values sent between devices are 32-bit elements; how exact they have to be, the bound alone decides.
No kernel may reach another device: no remote copies, remote signals or barrier semaphores. Data moves between devices by JAX's collectives and lax.ppermute only.
A program may use at most 64 MiB of HBM per device.

v0:
```python
import jax
import jax.numpy as jnp
import numpy as np
from jax import lax
from jax.experimental import pallas as pl
from jax.experimental.pallas import tpu as pltpu
from jax.sharding import Mesh, PartitionSpec as P

F32 = jnp.float32
BF16 = jnp.bfloat16
EXACT = lax.Precision.HIGHEST
NY, NZ = 1536, 8192
WALLS, STRIPS = 8, 64
PAIRS, PEERS = STRIPS // 2, 2 * WALLS
ROWS, COLS = NY // WALLS, NZ // STRIPS
OWNED = NY // PEERS
CHUNK = 10
SINE_Z, ENDS, EDGES, PICK, BOX_ROWS = 384, 512, 528, 544, 560
GHOST, MU_ROW, MU_COL, CLASS_ROWS = 0, 32, 40, 168
SPREAD, MIX_ROWS = 32, 160
PHI, LAM_ROW, ENDS_Z, ENDS_Y, SHARED_ROWS = 128, 136, 144, 152, 160


def halves(table):
    high = table.astype(np.float32).astype(BF16).astype(np.float64)
    return high, table - high


def sine_table(n):
    i = np.arange(1, n + 1)
    return np.sqrt(2 / (n + 1)) * np.sin(np.pi * np.outer(i, i) / (n + 1)), 4 * np.sin(np.pi * i / (2 * (n + 1))) ** 2


def tables():
    sine_y, mu_box = sine_table(ROWS)
    sine_z, lam = sine_table(COLS)
    ends_y, ends_z = sine_y[[0, -1]], sine_z[[0, -1]]
    boxes = np.zeros((BOX_ROWS, 256))
    boxes[:ROWS, :ROWS], boxes[ROWS:SINE_Z, :ROWS] = halves(sine_y)
    boxes[SINE_Z:ENDS, :COLS], boxes[SINE_Z:ENDS, COLS:] = halves(sine_z)
    boxes[ENDS : ENDS + 2, :ROWS], boxes[ENDS + 8 : ENDS + 10, :ROWS] = halves(ends_y)
    boxes[EDGES : EDGES + 2, :COLS], boxes[EDGES + 8 : EDGES + 10, :COLS] = halves(ends_z)
    boxes[PICK, 0], boxes[PICK + 1, COLS - 1] = -0.5, 0.5
    both = mu_box[:, None] + lam[None, :]
    shared = np.zeros((SHARED_ROWS, 256))
    shared[:PHI, :ROWS] = both.T
    shared[:PHI, ROWS:] = 1.0
    shared[PHI:LAM_ROW, :ROWS] = ends_y[0]
    shared[LAM_ROW:ENDS_Z, :COLS] = lam
    shared[ENDS_Z : ENDS_Z + 2, :COLS] = ends_z
    shared[ENDS_Y : ENDS_Y + 2, :ROWS] = ends_y
    r, wall = np.arange(ROWS), np.arange(WALLS)
    known = np.zeros((PEERS, CLASS_ROWS, COLS))
    mix = np.zeros((PEERS, MIX_ROWS, COLS))
    into = np.zeros((PEERS, 512, 256))
    back = np.zeros((PEERS, COLS, 1024))
    for c in range(PEERS):
        mode = c + PEERS * np.arange(OWNED)
        norm = np.where(mode == 0, np.sqrt(1 / NY), np.sqrt(2 / NY))
        angle = np.pi * np.outer(2 * r + 1, mode) / (2 * NY)
        turn = np.pi * c * wall / 8
        for k, wave in enumerate((np.cos(angle), np.sin(angle))):
            table = np.zeros((ROWS, COLS))
            table[:, :OWNED] = sine_y @ (norm * wave)
            high, low = halves(table)
            into[c, 256 * k : 256 * k + ROWS, :COLS], into[c, 256 * k : 256 * k + ROWS, COLS:] = high, low
            back[c, :, 256 * k : 256 * k + ROWS], back[c, :, 512 + 256 * k : 512 + 256 * k + ROWS] = high.T, low.T
        fold, spread = np.zeros((16, 64)), np.zeros((64, 16))
        for line in range(4):
            for core in range(2):
                box = 16 * line + 8 * core + wall
                fold[2 * line + core, box], fold[8 + 2 * line + core, box] = np.cos(turn), -np.sin(turn)
                spread[box, 2 * line + core], spread[box, 8 + 2 * line + core] = np.cos(turn), -np.sin(turn)
        mix[c, :16, :64], mix[c, 16:SPREAD, :64] = halves(fold)
        mix[c, SPREAD : SPREAD + 64, :16], mix[c, SPREAD + 64 :, :16] = halves(spread)
        for g in range(2):
            y = ROWS * (wall + g) + g - 1
            row = norm * np.cos(np.pi * np.outer(2 * y + 1, mode) / (2 * NY))
            for core in range(2):
                known[c, 16 * g + 8 * core : 16 * g + 8 * core + 8, :OWNED] = row
        mu = np.ones(COLS)
        mu[:OWNED] = 4 * np.sin(np.pi * mode / (2 * NY)) ** 2
        known[c, MU_ROW:MU_COL], known[c, MU_COL:] = mu, mu[:, None]
    whole = dict(both=both, shared=shared, known=known)
    half = dict(boxes=boxes, mix=mix, into=into, back=back)
    return {k: np.asarray(v, np.float32) for k, v in whole.items()}, {k: np.asarray(v, np.float32) for k, v in half.items()}


def dot(a, b, dims):
    return lax.dot_general(a, b, (dims, ((), ())), precision=EXACT, preferred_element_type=F32)


def fast(a, b, dims=((1,), (0,))):
    return lax.dot_general(a, b, (dims, ((), ())), preferred_element_type=F32)


def ids(shape, dim):
    return lax.broadcasted_iota(jnp.int32, shape, dim)


def pieces(value):
    high = value.astype(BF16).astype(F32)
    return high, value - high


def parts(value):
    return [piece.astype(BF16) for piece in pieces(value)]


def stacked(value):
    return jnp.concatenate(pieces(value), 0).astype(BF16)


def beside(value):
    return jnp.concatenate(parts(value), 1)


def joined(product, rows, width=COLS, at=0):
    here, other = slice(at, at + width), slice(at + width, at + 2 * width)
    return product[:rows, here] + (product[:rows, other] + product[rows:, here])


def start(pairs, sems):
    copies = [pltpu.make_async_copy(*pair, sems.at[i]) for i, pair in enumerate(pairs)]
    for copy in copies:
        copy.start()
    return copies


def pack(lines):
    tails = [jnp.concatenate([lines[side][:, COLS:ROWS], lines[2 + side][:, COLS:ROWS]], 1) for side in range(2)]
    return [line[:, :COLS] for line in lines] + tails


def unpack(rows):
    return [
        jnp.concatenate([rows[2 * plane + side], rows[4 + side][:, 64 * plane : 64 * plane + 64]], 1)
        for plane in range(2) for side in range(2)
    ]


def box_kernel(
    wave_hbm, vel_hbm, both_hbm, boxes_hbm,
    out_ref, freq_ref, solve_ref, boxes_ref,
    wave_ref, vel_ref, both_ref, sems,
):
    copies = start([
        (wave_hbm, wave_ref), (both_hbm, both_ref), (vel_hbm.at[:, 0], vel_ref.at[:, 0]),
        (vel_hbm.at[:, 1], vel_ref.at[:, 1]), (boxes_hbm, boxes_ref),
    ], sems)
    row, lane = ids((ROWS, COLS), 0), ids((ROWS, COLS), 1)
    wall = lax.axis_index("wall")
    low = jnp.where(wall > 0, -0.5, 0.0)
    high = jnp.where(wall < WALLS - 1, 0.5, 0.0)
    copies[0].wait()
    copies[1].wait()
    for plane in range(2):
        wave = wave_ref[plane]
        solve_ref[ROWS * plane : ROWS * (plane + 1), :] = -1.0 / (wave * wave + both_ref[...])
    sources, rims, sides = [], [], []
    for plane in range(2):
        copies[2 + plane].wait()
        u, v, w = (vel_ref[c, plane] for c in range(3))
        above = jnp.where(row == ROWS - 1, 0.0, pltpu.roll(v, ROWS - 1, 0))
        below = jnp.where(row == 0, 0.0, pltpu.roll(v, 1, 0))
        after = jnp.where(lane == COLS - 1, 0.0, pltpu.roll(w, COLS - 1, 1))
        before = jnp.where(lane == 0, 0.0, pltpu.roll(w, 1, 1))
        sources += parts(wave_ref[plane] * u + 0.5 * ((above - below) + (after - before)))
        rims += [low * v[0:1], high * v[ROWS - 1 :]]
        sides.append(parts(w))
    copies[4].wait()
    sine, sine_z = boxes_ref[:SINE_Z, :ROWS], boxes_ref[SINE_Z:ENDS, :]
    product = fast(sine, jnp.concatenate(sources, 1))
    product = fast(jnp.concatenate([stacked(joined(product, ROWS, at=256 * p)) for p in range(2)], 0), sine_z)
    insides = []
    for plane in range(2):
        freq = joined(product[2 * ROWS * plane : 2 * ROWS * (plane + 1)], ROWS)
        rows = slice(ROWS * plane, ROWS * (plane + 1))
        freq_ref[rows, :] = freq
        insides.append(parts(freq * solve_ref[rows, :]))
    pick, edge = boxes_ref[PICK:BOX_ROWS, :COLS], boxes_ref[EDGES:PICK, :COLS]
    across = ((1,), (1,))
    halo = [(fast(pick, high, across) + fast(pick, low, across))[0:2] for high, low in sides]
    halo = stacked(jnp.concatenate(halo + [jnp.zeros((4, ROWS), F32)], 0))
    left, right = fast(halo, boxes_ref[:ROWS, :]), fast(halo, boxes_ref[ROWS:SINE_Z, :])
    halo = (left[0:8] + (left[8:16] + right[0:8]))[:, :ROWS]
    lines = []
    for plane, (high, low) in enumerate(insides):
        left, right = fast(edge, high, across), fast(edge, low, across)
        line = left[0:2] + (left[8:10] + right[0:2]) + halo[2 * plane : 2 * plane + 2]
        lines += [line[0:1], line[1:2]]
    ends = fast(boxes_ref[ENDS:EDGES, :ROWS], jnp.concatenate(insides[0] + insides[1], 1))
    ends = [joined(ends, 8, at=256 * p)[0:2] for p in range(2)]
    rims = fast(stacked(jnp.concatenate(rims + [jnp.zeros((4, COLS), F32)], 0)), sine_z)
    ends = jnp.concatenate(ends, 0) + joined(rims, 8)[0:4]
    four = jnp.concatenate((pack(lines) + [ends]) * 4, 0)
    for group in range(PEERS // 4):
        out_ref[4 * CHUNK * group : 4 * CHUNK * (group + 1), :] = four


def decay(shift):
    root = jnp.sqrt(shift * (shift + 4.0))
    delta = (shift + root) / (2.0 + shift + root)
    return 1.0 - delta, delta * (2.0 - delta), -jnp.log1p(-delta)


def factor_kernel(
    wave_hbm, shared_hbm, known_hbm, mix_hbm, into_hbm, back_hbm,
    chain_ref, reach_ref, cauchy_ref, ring_ref, pair_ref, shared_ref, known_ref, mix_ref, into_ref, back_ref,
    wave_ref, sems,
):
    pair, mine = lax.axis_index("pair"), 8 * lax.axis_index("core") + lax.axis_index("wall")
    copies = start([
        (wave_hbm, wave_ref), (shared_hbm, shared_ref), (known_hbm.at[mine], known_ref), (mix_hbm.at[mine], mix_ref),
        (into_hbm.at[mine], into_ref), (back_hbm.at[mine], back_ref),
    ], sems)
    for copy in copies[:3]:
        copy.wait()
    waves = [wave_ref[p] * wave_ref[p] for p in range(2)]
    row = ids((8, COLS), 0)
    lam = shared_ref[LAM_ROW:ENDS_Z, :COLS]
    for p in range(2):
        at = COLS * p
        reach_ref[at : at + COLS, :] = beside(shared_ref[PHI : PHI + 1, :] / (waves[p] + shared_ref[:PHI, :]))
        cauchy_ref[at : at + COLS, :] = beside(1.0 / (known_ref[MU_COL:, :] + (waves[p] + lam[0:1])))
        rho, gap, theta = decay(waves[p] + lam)
        step = -1.0 * ROWS * theta
        scale = 1.0 / (gap * (1.0 - jnp.exp(-2.0 * NY * theta)))
        cross = jnp.exp(-(ROWS + 1.0) * theta)

        def reach(n):
            return jnp.exp(step * lax.bitwise_and(n, 15).astype(F32))

        for other in range(WALLS):
            up, down = reach(row - 1 - other) + rho * reach(15 - row - other), reach(row + other) + rho * reach(other - row)
            at = 32 * (WALLS * p + other)
            chain_ref[at : at + 8, :] = scale * (cross * up + down)
            chain_ref[at + 8 : at + 16, :] = scale * (up + cross * down)
            up, down = rho * reach(row - other) + reach(14 - row - other), rho * reach(row + 1 + other) + reach(other - row - 1)
            chain_ref[at + 16 : at + 24, :] = scale * (cross * up + down)
            chain_ref[at + 24 : at + 32, :] = scale * (up + cross * down)
    rho, gap, theta = decay(jnp.where(row >= 4, waves[1], waves[0]) + known_ref[MU_ROW:MU_COL, :])
    pair_ref[0:8, :] = jnp.exp(-(COLS + 1.0) * theta)
    pair_ref[8:16, :] = jnp.exp(-1.0 * COLS * theta)
    step = -2.0 * COLS * theta
    leftward = row % 2 == 0
    swapped = jnp.concatenate([step[0:2], step[4:6]] * 2, 0)
    for group in range(PAIRS // 2):
        other = 2 * group + row // 4
        n = lax.bitwise_and(jnp.where(leftward, other - pair - 1, pair - 1 - other), PAIRS - 1)
        ring_ref[8 * group : 8 * group + 8, :] = jnp.exp(swapped * n.astype(F32))
    period = 1.0 - jnp.exp(-1.0 * NZ * theta)
    for i, value in enumerate((rho, 1.0 / (gap * period), period, jnp.exp(-1.0 * COLS * theta))):
        pair_ref[16 + 8 * i : 24 + 8 * i, :] = jnp.concatenate([value[0:1], value[4:5]] * 4, 0)
    for copy in copies[3:]:
        copy.wait()


def strip_kernel(in_ref, chain_ref, reach_ref, pair_ref, shared_ref, mix_ref, into_ref, out_ref, own_ref, sums_ref, near_ref):
    box = [in_ref[pl.ds(i, PEERS, stride=CHUNK), :] for i in range(6)]
    ends = shared_ref[ENDS_Z : ENDS_Z + 2, :COLS]
    lines = unpack(box)
    even = ids((2 * PEERS, ROWS), 1) % 2 == 0
    added = []
    for plane in range(2):
        tops, bottoms = [], []
        for core in range(2):
            top = bottom = None
            for other in range(WALLS):
                at = 32 * (WALLS * plane + other)
                source = CHUNK * (WALLS * core + other) + 6 + 2 * plane
                first, last = in_ref[source : source + 1, :], in_ref[source + 1 : source + 2, :]
                weight = [chain_ref[at + 8 * i : at + 8 * i + 8, :] for i in range(4)]
                one, two = weight[0] * first + weight[1] * last, weight[2] * first + weight[3] * last
                top, bottom = (one, two) if top is None else (top + one, bottom + two)
            tops.append(top)
            bottoms.append(bottom)
        top, bottom = jnp.concatenate(tops, 0), jnp.concatenate(bottoms, 0)
        near_ref[pl.ds(2 * plane, PEERS, stride=8), :] = top
        near_ref[pl.ds(2 * plane + 1, PEERS, stride=8), :] = bottom
        sums = [value * ends[side : side + 1] for value in (top + bottom, top - bottom) for side in range(2)]
        product = fast(stacked(jnp.concatenate(sums, 0)), reach_ref[COLS * plane : COLS * (plane + 1), :])
        product = joined(product, 4 * PEERS, 256)[:, :ROWS]
        added.append(jnp.where(even, product[: 2 * PEERS], product[2 * PEERS :]))
    mine = 8 * lax.axis_index("core") + lax.axis_index("wall")
    own_ref[...] = near_ref[pl.ds(pl.multiple_of(8 * mine, 8), 8), :]
    lines = jnp.concatenate(lines, 0) + jnp.concatenate(added, 0)
    lines = jnp.concatenate([lines, jnp.zeros((4 * PEERS, 256 - ROWS), F32)], 1)
    folded = joined(fast(mix_ref[:SPREAD, :64], beside(lines)), 16, 256)
    folded = stacked(jnp.concatenate([folded[0:8], folded[8:16]], 1))
    modes = joined(fast(folded, into_ref[...]), 8)
    row = ids((8, COLS), 0)
    modes = modes + pair_ref[0:8, :] * jnp.where(row % 4 < 2, pltpu.roll(modes, 6, 0), pltpu.roll(modes, 2, 0))
    sums_ref[...] = modes
    modes = modes + pair_ref[8:16, :] * jnp.where(row % 2 == 0, pltpu.roll(modes, 7, 0), pltpu.roll(modes, 1, 0))
    out = jnp.concatenate([modes[0:1], modes[3:4], modes[4:5], modes[7:8]] * 2, 0)
    for group in range(PAIRS // 2):
        out_ref[8 * group : 8 * group + 8, :] = out


def ring_kernel(in_ref, sums_ref, ring_ref, pair_ref, known_ref, mix_ref, back_ref, cauchy_ref, shared_ref, out_ref):
    total = in_ref[0:8, :] * ring_ref[0:8, :]
    for group in range(1, PAIRS // 2):
        total = total + in_ref[8 * group : 8 * group + 8, :] * ring_ref[8 * group : 8 * group + 8, :]
    total = total[0:4] + total[4:8]
    rho, scale, period, block = (pair_ref[16 + 8 * i : 18 + 8 * i, :] for i in range(4))

    def planes(value, at, step):
        return jnp.concatenate([value[at : at + 1], value[at + step : at + step + 1]], 0)

    after, before = planes(total, 0, 2), planes(total, 1, 2)
    left0, left1, right0, right1 = (period * planes(sums_ref, i, 4) for i in range(4))
    coming, going = block * before + right0, block * after + left1
    left = [scale * (before + rho * (left0 + block * going)), scale * (coming + rho * going)]
    right = [scale * (rho * coming + going), scale * (rho * (right1 + block * coming) + after)]
    ghosts = [[side[p : p + 1] for side in left + right] for p in range(2)]
    cells = joined(fast(stacked(jnp.concatenate(ghosts[0] + ghosts[1], 0)), back_ref[...]), 8, 512)
    cells = jnp.concatenate([cells[:, :256], cells[:, 256:]], 0)
    cells = joined(fast(mix_ref[SPREAD:, :16], beside(cells)), 64, 256)
    for i, value in enumerate(pack([cells[PEERS * i : PEERS * (i + 1)] for i in range(4)])):
        out_ref[pl.ds(i, PEERS, stride=CHUNK), :] = value
    ends = shared_ref[ENDS_Z : ENDS_Z + 2, :COLS]
    known = known_ref[GHOST:MU_ROW, :]
    is_first = ids((32, COLS), 0) % 16 < 8
    for plane in range(2):
        both = [known * jnp.where(is_first, ghosts[plane][2 * side], ghosts[plane][2 * side + 1]) for side in range(2)]
        rims = joined(fast(stacked(jnp.concatenate(both, 0)), cauchy_ref[COLS * plane : COLS * (plane + 1), :]), 64)
        rims = rims[:32] * ends[0:1] + rims[32:] * ends[1:2]
        for side in range(2):
            out_ref[pl.ds(6 + 2 * plane + side, PEERS, stride=CHUNK), :] = rims[PEERS * side : PEERS * (side + 1)]


def final_kernel(in_ref, own_ref, freq_ref, solve_ref, boxes_ref, shared_ref, out_ref):
    step = 4 * CHUNK
    total = (in_ref[0:step, :] + in_ref[step : 2 * step, :]) + (in_ref[2 * step : 3 * step, :] + in_ref[3 * step :, :])
    total = (total[0:CHUNK] + total[CHUNK : 2 * CHUNK]) + (total[2 * CHUNK : 3 * CHUNK] + total[3 * CHUNK :])
    sides = unpack([total[i : i + 1] for i in range(6)])
    rims = total[6:10] + own_ref[0:4, :]
    sine, sine_z = boxes_ref[:SINE_Z, :ROWS], boxes_ref[SINE_Z:ENDS, :]
    freqs = []
    for plane in range(2):
        rows = slice(ROWS * plane, ROWS * (plane + 1))
        lhs = [shared_ref[ENDS_Y : ENDS_Y + 2, :ROWS]] + sides[2 * plane : 2 * plane + 2] + [jnp.zeros((4, ROWS), F32)]
        rhs = [rims[2 * plane : 2 * plane + 2], shared_ref[ENDS_Z : ENDS_Z + 2, :COLS], jnp.zeros((4, COLS), F32)]
        change = dot(jnp.concatenate(lhs, 0), jnp.concatenate(rhs, 0), ((0,), (0,)))
        freqs.append(stacked((freq_ref[rows, :] - change) * solve_ref[rows, :]))
    product = fast(jnp.concatenate(freqs, 0), sine_z)
    lines = [beside(joined(product[2 * ROWS * p : 2 * ROWS * (p + 1)], ROWS)) for p in range(2)]
    product = fast(sine, jnp.concatenate(lines, 1))
    for plane in range(2):
        out_ref[plane] = joined(product, ROWS, at=256 * plane)


VMEM = pl.BlockSpec(memory_space=pltpu.VMEM)
HBM = pl.BlockSpec(memory_space=pltpu.HBM)


def call(kernel, shapes, specs, *operands, scratch=()):
    outs = [jax.ShapeDtypeStruct(s[0], s[1]) if isinstance(s[0], tuple) else jax.ShapeDtypeStruct(s, F32) for s in shapes]
    operands = [pltpu.with_memory_space_constraint(x, pltpu.HBM) if s is HBM else x for s, x in zip(specs, operands)]
    return pl.pallas_call(
        kernel,
        out_shape=outs if len(outs) > 1 else outs[0],
        in_specs=specs,
        out_specs=[VMEM] * len(outs) if len(outs) > 1 else VMEM,
        scratch_shapes=list(scratch),
        compiler_params=pltpu.CompilerParams(vmem_limit_bytes=24 << 20),
    )(*operands)


def exchange(block, axes):
    return lax.all_to_all(block, axes, split_axis=0, concat_axis=0, tiled=True)


def on_device(velocity, wave_x):
    whole, half = tables()
    t = {k: jnp.asarray(v) for k, v in whole.items()} | {k: jnp.asarray(v, BF16) for k, v in half.items()}
    pltpu_smem = pltpu.SMEM((2,), F32)
    sent, freq, solve, boxes = call(
        box_kernel, [(PEERS * CHUNK, COLS), (2 * ROWS, COLS), (2 * ROWS, COLS), ((BOX_ROWS, 256), BF16)],
        [HBM] * 4, wave_x, velocity, t["both"], t["boxes"],
        scratch=[
            pltpu_smem, pltpu.VMEM((3, 2, ROWS, COLS), F32), pltpu.VMEM((ROWS, COLS), F32), pltpu.SemaphoreType.DMA((5,)),
        ],
    )
    chain, reach, cauchy, ring, pair, shared, known, mix, into, back = call(
        factor_kernel,
        [
            (64 * WALLS, COLS), ((2 * COLS, 512), BF16), ((2 * COLS, 256), BF16), (4 * PAIRS, COLS), (48, COLS),
            (SHARED_ROWS, 256), (CLASS_ROWS, COLS), ((MIX_ROWS, COLS), BF16), ((512, 256), BF16), ((COLS, 1024), BF16),
        ],
        [HBM] * 6, wave_x, t["shared"], t["known"], t["mix"], t["into"], t["back"],
        scratch=[pltpu_smem, pltpu.SemaphoreType.DMA((6,))],
    )
    half_chunk = (PEERS * CHUNK // 2, 2, COLS)
    sent = exchange(sent.reshape(half_chunk), ("core", "wall")).reshape(PEERS * CHUNK, COLS)
    modes, own, sums = call(
        strip_kernel, [(4 * PAIRS, COLS), (8, COLS), (8, COLS)], [VMEM] * 7,
        sent, chain, reach, pair, shared, mix, into, scratch=[pltpu.VMEM((8 * PEERS, COLS), F32)],
    )
    modes = exchange(modes.reshape(PAIRS, 4, COLS), "pair").reshape(4 * PAIRS, COLS)
    cells = call(
        ring_kernel, [(PEERS * CHUNK, COLS)], [VMEM] * 9, modes, sums, ring, pair, known, mix, back, cauchy, shared
    )
    cells = exchange(cells.reshape(half_chunk), ("core", "wall")).reshape(PEERS * CHUNK, COLS)
    return call(final_kernel, [(2, ROWS, COLS)], [VMEM] * 6, cells, own, freq, solve, boxes, shared)


def solution(mesh):
    fine = Mesh(mesh.devices.reshape(PAIRS, 2, WALLS), ("pair", "core", "wall"))
    placed = (P(None, None, "wall", ("pair", "core")), P())
    return jax.shard_map(
        on_device, mesh=fine, in_specs=placed, out_specs=P(None, "wall", ("pair", "core")), check_vma=False
    )
```

profile of v0, /device:TPU:1, one launch (start us, length us, event | category | flops | bytes accessed | tf_op | source)
XLA Modules:
  0.0 54.9 jit_solution(436535006217089454)
XLA Ops:
  0.0 2.7 %shard_map.91 = (f32[160,128]{1,0:T(8,128)}, f32[384,128]{1,0:T(8,128)S(1)}, f32[384,128]{1,0:T(8,128)S(1)}, bf16[560,256]{1,0:T(8,128)(2,1)S(1)}) custom-call(f32[2]{0:T(128)} %wave_hbm.3, f32[3,2,192,128]{3,2,1,0:T(8,128)} %vel_hbm.1, f32[192,128]{1,0:T(8,128)} %constant.14.clone.both_hbm, bf16[560,256]{1,0:T(8,128)(2,1)} %constant.17.clone.boxes_hbm), custom_call_target="tpu_custom_call" | custom-call | tf_op jit(solution)/shard_map/pallas_call | solution.py:361
  2.7 10.2 %all-to-all-start = ((f32[80,2,128]{2,1,0:T(2,128)}), f32[80,2,128]{2,1,0:T(2,128)S(1)}, u32[]{:S(2)}, u32[]{:S(2)}) async-start(f32[80,2,128]{2,1,0:T(2,128)} %bitcast), calls=%async_computation | async-start | bytes 163840 | tf_op jit(solution)/shard_map/all_to_all | solution.py:372
  12.9 1.3 %shard_map.92 = (f32[512,128]{1,0:T(8,128)S(1)}, bf16[256,512]{1,0:T(8,128)(2,1)S(1)}, bf16[256,256]{1,0:T(8,128)(2,1)S(1)}, f32[128,128]{1,0:T(8,128)S(1)}, f32...) custom-call(f32[2]{0:T(128)} %wave_hbm.3, ...), custom_call_target="tpu_custom_call" | custom-call | tf_op jit(solution)/shard_map/pallas_call | solution.py:361
  14.2 6.0 %all-to-all-done = f32[80,2,128]{2,1,0:T(2,128)S(1)} async-done(((f32[80,2,128]{2,1,0:T(2,128)}), f32[80,2,128]{2,1,0:T(2,128)S(1)}, u32[]{:S(2)}, u32[]{:S(2)}) %all-to-all-start) | async-done | bytes 81952 | tf_op jit(solution)/shard_map/all_to_all | solution.py:372
  20.2 0.6 %shard_map.93 = (f32[128,128]{1,0:T(8,128)S(1)}, f32[8,128]{1,0:T(8,128)S(1)}, f32[8,128]{1,0:T(8,128)S(1)}) custom-call(f32[160,128]{1,0:T(8,128)S(1)} %bitcast.6, f32[512,128]{1,0:T(8,128)S(1)} %get-tuple-element.23.chain_ref, bf16[256,512]{1,0:T(8,128)(2,1)S(1)} %get-tuple-element.24.reach_ref, f32[48,128]{1,0:T(8,128)S(1)} %get-tuple-element.25.pair_ref, ...), custom_call_target="tpu_custom_call" | custom-call | tf_op jit(solution)/shard_map/pallas_call | solution.py:361
  20.7 20.0 %all_to_all.15 = f32[32,4,128]{2,1,0:T(4,128)S(1)} all-to-all(f32[32,4,128]{2,1,0:T(4,128)S(1)} %bitcast.10), channel_id=1, replica_groups=mesh['pair'=32,'core'=2,'wall'=8] {'pair'}, dimensions={0} | all-to-all | bytes 131072 | tf_op jit(solution)/shard_map/all_to_all | solution.py:372
  40.7 0.4 shard_map.94
  41.2 12.1 %all_to_all.16 = f32[80,2,128]{2,1,0:T(2,128)S(1)} all-to-all(f32[80,2,128]{2,1,0:T(2,128)S(1)} %bitcast.8), channel_id=1, replica_groups=mesh['pair'=32,'core'=2,'wall'=8] {'core','wall'}, dimensions={0} | all-to-all | bytes 163840 | tf_op jit(solution)/shard_map/all_to_all | solution.py:372
  53.3 1.6 %shard_map.95 = f32[2,192,128]{2,1,0:T(8,128)} custom-call(f32[160,128]{1,0:T(8,128)S(1)} %bitcast.7, f32[8,128]{1,0:T(8,128)S(1)} %get-tuple-element.35.own_ref, f32[384,128]{1,0:T(8,128)S(1)} %get-tuple-element.36.freq_ref, f32[384,128]{1,0:T(8,128)S(1)} %get-tuple-element.37.solve_ref, bf16[560,256]{1,0:T(8,128)(2,1)S(1)} %get-tuple-element.38.boxes_ref, ...), custom_call_target="tpu_custom_call" | custom-call | tf_op jit(solution)/shard_map/pallas_call | solution.py:361
Async XLA Ops:
  2.7 17.5 %all-to-all-start = ((f32[80,2,128]{2,1,0:T(2,128)}), f32[80,2,128]{2,1,0:T(2,128)S(1)}, u32[]{:S(2)}, u32[]{:S(2)}) async-start(f32[80,2,128]{2,1,0:T(2,128)} %bitcast), calls=%async_computation | async-start | bytes 163840 | tf_op jit(solution)/shard_map/all_to_all | solution.py:372
where the time goes:
time: 55.1 us; the launch traced here: 54.9 us
  blocking collectives  32.1 us (58%)
  starting transfers between devices  10.2 us (19%)
  Pallas kernels  6.53 us (12%)
  waiting for transfers between devices  5.95 us (11%)
    all_to_all x2, blocking collectives, exchange(): return lax.all_to_all(block, axes, split_axis=0, concat_axis=0, tiled=True)  32.1 us
    all_to_all x1, starting transfers between devices, exchange(): return lax.all_to_all(block, axes, split_axis=0, concat_axis=0, tiled=True)  10.2 us
    pallas_call x5, Pallas kernels, call(): pl.pallas_call(kernel, out_shape=outs if len(outs) > 1 else outs[0], in_s...  6.53 us
    all_to_all x1, waiting for transfers between devices, exchange(): return lax.all_to_all(block, axes, split_axis=0, concat_axis=0, tiled=True)  5.95 us
  transfers between devices with their start and end apart: 1, of which 1 were waited for; matrix products, arithmetic and copies ran while one was open for 0% of the time, Pallas kernels for 2%

commit v1 on v0

--- a/solution.py
+++ b/solution.py
@@ -18,7 +18,7 @@
 SINE_Z, ENDS, EDGES, PICK, BOX_ROWS = 384, 512, 528, 544, 560
 GHOST, MU_ROW, MU_COL, CLASS_ROWS = 0, 32, 40, 168
 SPREAD, MIX_ROWS = 32, 160
-PHI, LAM_ROW, ENDS_Z, ENDS_Y, SHARED_ROWS = 128, 136, 144, 152, 160
+PHI, LAM_ROW, ENDS_Z, MU_BOX, SHARED_ROWS = 128, 136, 144, 152, 160
 
 
 def halves(table):
@@ -48,7 +48,8 @@
     shared[PHI:LAM_ROW, :ROWS] = ends_y[0]
     shared[LAM_ROW:ENDS_Z, :COLS] = lam
     shared[ENDS_Z : ENDS_Z + 2, :COLS] = ends_z
-    shared[ENDS_Y : ENDS_Y + 2, :ROWS] = ends_y
+    shared[MU_BOX:] = 1.0
+    shared[MU_BOX:, :ROWS] = mu_box
     r, wall = np.arange(ROWS), np.arange(WALLS)
     known = np.zeros((PEERS, CLASS_ROWS, COLS))
     mix = np.zeros((PEERS, MIX_ROWS, COLS))
@@ -141,8 +142,8 @@
 
 def box_kernel(
     wave_hbm, vel_hbm, both_hbm, boxes_hbm,
-    out_ref, freq_ref, solve_ref, boxes_ref,
-    wave_ref, vel_ref, both_ref, sems,
+    out_ref, inside_ref, boxes_ref,
+    wave_ref, vel_ref, both_ref, solve_ref, sems,
 ):
     copies = start([
         (wave_hbm, wave_ref), (both_hbm, both_ref), (vel_hbm.at[:, 0], vel_ref.at[:, 0]),
@@ -176,8 +177,9 @@
     for plane in range(2):
         freq = joined(product[2 * ROWS * plane : 2 * ROWS * (plane + 1)], ROWS)
         rows = slice(ROWS * plane, ROWS * (plane + 1))
-        freq_ref[rows, :] = freq
-        insides.append(parts(freq * solve_ref[rows, :]))
+        inside = freq * solve_ref[rows, :]
+        inside_ref[rows, :] = inside
+        insides.append(parts(inside))
     pick, edge = boxes_ref[PICK:BOX_ROWS, :COLS], boxes_ref[EDGES:PICK, :COLS]
     across = ((1,), (1,))
     halo = [(fast(pick, high, across) + fast(pick, low, across))[0:2] for high, low in sides]
@@ -205,8 +207,9 @@
 
 
 def factor_kernel(
-    wave_hbm, shared_hbm, known_hbm, mix_hbm, into_hbm, back_hbm,
+    wave_hbm, shared_hbm, known_hbm, mix_hbm, into_hbm, back_hbm, inside_ref, boxes_ref,
     chain_ref, reach_ref, cauchy_ref, ring_ref, pair_ref, shared_ref, known_ref, mix_ref, into_ref, back_ref,
+    base_ref, down_ref, across_ref,
     wave_ref, sems,
 ):
     pair, mine = lax.axis_index("pair"), 8 * lax.axis_index("core") + lax.axis_index("wall")
@@ -252,6 +255,22 @@
     period = 1.0 - jnp.exp(-1.0 * NZ * theta)
     for i, value in enumerate((rho, 1.0 / (gap * period), period, jnp.exp(-1.0 * COLS * theta))):
         pair_ref[16 + 8 * i : 24 + 8 * i, :] = jnp.concatenate([value[0:1], value[4:5]] * 4, 0)
+    sine, sine_z = boxes_ref[:SINE_Z, :ROWS], boxes_ref[SINE_Z:ENDS, :]
+    product = fast(jnp.concatenate([stacked(inside_ref[ROWS * p : ROWS * (p + 1), :]) for p in range(2)], 0), sine_z)
+    lines = [beside(joined(product[2 * ROWS * p : 2 * ROWS * (p + 1)], ROWS)) for p in range(2)]
+    product = fast(sine, jnp.concatenate(lines, 1))
+    for plane in range(2):
+        base_ref[ROWS * plane : ROWS * (plane + 1), :] = joined(product, ROWS, at=256 * plane)
+        for ref, shift, count in (
+            (down_ref, shared_ref[LAM_ROW : LAM_ROW + 1, :COLS], ROWS), (across_ref, shared_ref[MU_BOX : MU_BOX + 1, :], COLS),
+        ):
+            _, _, theta = decay(waves[plane] + shift)
+            whole = 1.0 / (1.0 - jnp.exp(-2.0 * (count + 1) * theta))
+            step = ids((count, shift.shape[1]), 0).astype(F32)
+            for side in range(2):
+                n = step if side == 0 else count - 1.0 - step
+                at = count * (2 * plane + side)
+                ref[at : at + count, :] = jnp.exp(-(n + 1.0) * theta) * (1.0 - jnp.exp(-2.0 * (count - n) * theta)) * whole
     for copy in copies[3:]:
         copy.wait()
 
@@ -330,39 +349,40 @@
             out_ref[pl.ds(6 + 2 * plane + side, PEERS, stride=CHUNK), :] = rims[PEERS * side : PEERS * (side + 1)]
 
 
-def final_kernel(in_ref, own_ref, freq_ref, solve_ref, boxes_ref, shared_ref, out_ref):
+def final_kernel(in_ref, own_ref, base_ref, down_ref, across_ref, boxes_ref, out_hbm, out_ref, sems):
     step = 4 * CHUNK
     total = (in_ref[0:step, :] + in_ref[step : 2 * step, :]) + (in_ref[2 * step : 3 * step, :] + in_ref[3 * step :, :])
     total = (total[0:CHUNK] + total[CHUNK : 2 * CHUNK]) + (total[2 * CHUNK : 3 * CHUNK] + total[3 * CHUNK :])
     sides = unpack([total[i : i + 1] for i in range(6)])
     rims = total[6:10] + own_ref[0:4, :]
     sine, sine_z = boxes_ref[:SINE_Z, :ROWS], boxes_ref[SINE_Z:ENDS, :]
-    freqs = []
-    for plane in range(2):
-        rows = slice(ROWS * plane, ROWS * (plane + 1))
-        lhs = [shared_ref[ENDS_Y : ENDS_Y + 2, :ROWS]] + sides[2 * plane : 2 * plane + 2] + [jnp.zeros((4, ROWS), F32)]
-        rhs = [rims[2 * plane : 2 * plane + 2], shared_ref[ENDS_Z : ENDS_Z + 2, :COLS], jnp.zeros((4, COLS), F32)]
-        change = dot(jnp.concatenate(lhs, 0), jnp.concatenate(rhs, 0), ((0,), (0,)))
-        freqs.append(stacked((freq_ref[rows, :] - change) * solve_ref[rows, :]))
-    product = fast(jnp.concatenate(freqs, 0), sine_z)
-    lines = [beside(joined(product[2 * ROWS * p : 2 * ROWS * (p + 1)], ROWS)) for p in range(2)]
-    product = fast(sine, jnp.concatenate(lines, 1))
-    for plane in range(2):
-        out_ref[plane] = joined(product, ROWS, at=256 * plane)
+    copies = []
+    for plane in range(2):
+        down, across = [], []
+        for side in range(2):
+            at = 2 * plane + side
+            down.append(rims[at : at + 1] * down_ref[ROWS * at : ROWS * (at + 1), :])
+            across.append(sides[at] * across_ref[COLS * at : COLS * (at + 1), :ROWS])
+        down = joined(fast(stacked(down[0] + down[1]), sine_z), ROWS)
+        across = joined(fast(sine, stacked(across[0] + across[1]), ((1,), (1,))), ROWS)
+        out_ref[plane] = base_ref[ROWS * plane : ROWS * (plane + 1), :] + (down + across)
+        copies += start([(out_ref.at[plane], out_hbm.at[plane])], sems.at[pl.ds(plane, 1)])
+    for copy in copies:
+        copy.wait()
 
 
 VMEM = pl.BlockSpec(memory_space=pltpu.VMEM)
 HBM = pl.BlockSpec(memory_space=pltpu.HBM)
 
 
-def call(kernel, shapes, specs, *operands, scratch=()):
+def call(kernel, shapes, specs, *operands, scratch=(), into=VMEM):
     outs = [jax.ShapeDtypeStruct(s[0], s[1]) if isinstance(s[0], tuple) else jax.ShapeDtypeStruct(s, F32) for s in shapes]
     operands = [pltpu.with_memory_space_constraint(x, pltpu.HBM) if s is HBM else x for s, x in zip(specs, operands)]
     return pl.pallas_call(
         kernel,
         out_shape=outs if len(outs) > 1 else outs[0],
         in_specs=specs,
-        out_specs=[VMEM] * len(outs) if len(outs) > 1 else VMEM,
+        out_specs=[into] * len(outs) if len(outs) > 1 else into,
         scratch_shapes=list(scratch),
         compiler_params=pltpu.CompilerParams(vmem_limit_bytes=24 << 20),
     )(*operands)
@@ -376,20 +396,22 @@
     whole, half = tables()
     t = {k: jnp.asarray(v) for k, v in whole.items()} | {k: jnp.asarray(v, BF16) for k, v in half.items()}
     pltpu_smem = pltpu.SMEM((2,), F32)
-    sent, freq, solve, boxes = call(
-        box_kernel, [(PEERS * CHUNK, COLS), (2 * ROWS, COLS), (2 * ROWS, COLS), ((BOX_ROWS, 256), BF16)],
+    sent, inside, boxes = call(
+        box_kernel, [(PEERS * CHUNK, COLS), (2 * ROWS, COLS), ((BOX_ROWS, 256), BF16)],
         [HBM] * 4, wave_x, velocity, t["both"], t["boxes"],
         scratch=[
-            pltpu_smem, pltpu.VMEM((3, 2, ROWS, COLS), F32), pltpu.VMEM((ROWS, COLS), F32), pltpu.SemaphoreType.DMA((5,)),
+            pltpu_smem, pltpu.VMEM((3, 2, ROWS, COLS), F32), pltpu.VMEM((ROWS, COLS), F32),
+            pltpu.VMEM((2 * ROWS, COLS), F32), pltpu.SemaphoreType.DMA((5,)),
         ],
     )
-    chain, reach, cauchy, ring, pair, shared, known, mix, into, back = call(
+    chain, reach, cauchy, ring, pair, shared, known, mix, into, back, base, down, across = call(
         factor_kernel,
         [
             (64 * WALLS, COLS), ((2 * COLS, 512), BF16), ((2 * COLS, 256), BF16), (4 * PAIRS, COLS), (48, COLS),
             (SHARED_ROWS, 256), (CLASS_ROWS, COLS), ((MIX_ROWS, COLS), BF16), ((512, 256), BF16), ((COLS, 1024), BF16),
+            (2 * ROWS, COLS), (4 * ROWS, COLS), (4 * COLS, 256),
         ],
-        [HBM] * 6, wave_x, t["shared"], t["known"], t["mix"], t["into"], t["back"],
+        [HBM] * 6 + [VMEM] * 2, wave_x, t["shared"], t["known"], t["mix"], t["into"], t["back"], inside, boxes,
         scratch=[pltpu_smem, pltpu.SemaphoreType.DMA((6,))],
     )
     half_chunk = (PEERS * CHUNK // 2, 2, COLS)
@@ -403,7 +425,10 @@
         ring_kernel, [(PEERS * CHUNK, COLS)], [VMEM] * 9, modes, sums, ring, pair, known, mix, back, cauchy, shared
     )
     cells = exchange(cells.reshape(half_chunk), ("core", "wall")).reshape(PEERS * CHUNK, COLS)
-    return call(final_kernel, [(2, ROWS, COLS)], [VMEM] * 6, cells, own, freq, solve, boxes, shared)
+    return call(
+        final_kernel, [(2, ROWS, COLS)], [VMEM] * 6, cells, own, base, down, across, boxes,
+        scratch=[pltpu.VMEM((2, ROWS, COLS), F32), pltpu.SemaphoreType.DMA((2,))], into=HBM,
+    )
 
 
 def solution(mesh):

time: 55.1 us -> 54.6 us (level)
  waiting for transfers between devices: 5.95 us -> 5.19 us
    all_to_all x1, waiting for transfers between devices: 5.95 us -> 5.19 us  [exchange(): return lax.all_to_all(block, axes, split_axis=0, concat_axis=0, tiled=True)]
  transfers between devices with their start and end apart: 1 -> 1, of which waited for: 1 -> 1; matrix products, arithmetic and copies ran while one was open for 0% -> 0% of each run, Pallas kernels for 2% -> 4%
where the time goes in v1:
time: 54.6 us; the launch traced here: 54.3 us
  blocking collectives  32.1 us (59%)
  starting transfers between devices  10.2 us (19%)
  Pallas kernels  6.76 us (12%)
  waiting for transfers between devices  5.19 us (10%)
    all_to_all x2, blocking collectives, exchange(): return lax.all_to_all(block, axes, split_axis=0, concat_axis=0, tiled=True)  32.1 us
    all_to_all x1, starting transfers between devices, exchange(): return lax.all_to_all(block, axes, split_axis=0, concat_axis=0, tiled=True)  10.2 us
    pallas_call x5, Pallas kernels, call(): pl.pallas_call(kernel, out_shape=outs if len(outs) > 1 else outs[0], in_s...  6.76 us
    all_to_all x1, waiting for transfers between devices, exchange(): return lax.all_to_all(block, axes, split_axis=0, concat_axis=0, tiled=True)  5.19 us
  transfers between devices with their start and end apart: 1, of which 1 were waited for; matrix products, arithmetic and copies ran while one was open for 0% of the time, Pallas kernels for 4%

profile of v1, /device:TPU:1, one launch (start us, length us, event | category | flops | bytes accessed | tf_op | source)
XLA Modules:
  0.0 54.3 jit_solution(13546005427157009800)
XLA Ops:
  0.0 2.7 %shard_map.91 = (f32[160,128]{1,0:T(8,128)}, f32[384,128]{1,0:T(8,128)S(1)}, bf16[560,256]{1,0:T(8,128)(2,1)S(1)}) custom-call(f32[2]{0:T(128)} %wave_hbm.3, f32[3,2,192,128]{3,2,1,0:T(8,128)} %vel_hbm.1, f32[192,128]{1,0:T(8,128)} %constant.14.clone.both_hbm, bf16[560,256]{1,0:T(8,128)(2,1)} %constant.17.clone.boxes_hbm), custom_call_target="tpu_custom_call" | custom-call | tf_op jit(solution)/shard_map/pallas_call | solution.py:381
  2.7 10.2 %all-to-all-start = ((f32[80,2,128]{2,1,0:T(2,128)}), f32[80,2,128]{2,1,0:T(2,128)S(1)}, u32[]{:S(2)}, u32[]{:S(2)}) async-start(f32[80,2,128]{2,1,0:T(2,128)} %bitcast), calls=%async_computation | async-start | bytes 163840 | tf_op jit(solution)/shard_map/all_to_all | solution.py:392
  12.9 2.1 %shard_map.92 = (f32[512,128]{1,0:T(8,128)S(1)}, bf16[256,512]{1,0:T(8,128)(2,1)S(1)}, bf16[256,256]{1,0:T(8,128)(2,1)S(1)}, f32[128,128]{1,0:T(8,128)S(1)}, f32...) custom-call(f32[2]{0:T(128)} %wave_hbm.3, ...), custom_call_target="tpu_custom_call" | custom-call | tf_op jit(solution)/shard_map/pallas_call | solution.py:381
  15.0 5.2 %all-to-all-done = f32[80,2,128]{2,1,0:T(2,128)S(1)} async-done(((f32[80,2,128]{2,1,0:T(2,128)}), f32[80,2,128]{2,1,0:T(2,128)S(1)}, u32[]{:S(2)}, u32[]{:S(2)}) %all-to-all-start) | async-done | bytes 81952 | tf_op jit(solution)/shard_map/all_to_all | solution.py:392
  20.2 0.5 %shard_map.93 = (f32[128,128]{1,0:T(8,128)S(1)}, f32[8,128]{1,0:T(8,128)S(1)}, f32[8,128]{1,0:T(8,128)S(1)}) custom-call(f32[160,128]{1,0:T(8,128)S(1)} %bitcast.6, f32[512,128]{1,0:T(8,128)S(1)} %get-tuple-element.27.chain_ref, bf16[256,512]{1,0:T(8,128)(2,1)S(1)} %get-tuple-element.28.reach_ref, f32[48,128]{1,0:T(8,128)S(1)} %get-tuple-element.29.pair_ref, ...), custom_call_target="tpu_custom_call" | custom-call | tf_op jit(solution)/shard_map/pallas_call | solution.py:381
  20.7 20.0 %all_to_all.15 = f32[32,4,128]{2,1,0:T(4,128)S(1)} all-to-all(f32[32,4,128]{2,1,0:T(4,128)S(1)} %bitcast.10), channel_id=1, replica_groups=mesh['pair'=32,'core'=2,'wall'=8] {'pair'}, dimensions={0} | all-to-all | bytes 131072 | tf_op jit(solution)/shard_map/all_to_all | solution.py:392
  40.7 0.4 shard_map.94
  41.2 12.1 %all_to_all.16 = f32[80,2,128]{2,1,0:T(2,128)S(1)} all-to-all(f32[80,2,128]{2,1,0:T(2,128)S(1)} %bitcast.8), channel_id=1, replica_groups=mesh['pair'=32,'core'=2,'wall'=8] {'core','wall'}, dimensions={0} | all-to-all | bytes 163840 | tf_op jit(solution)/shard_map/all_to_all | solution.py:392
  53.3 1.1 %shard_map.95 = f32[2,192,128]{2,1,0:T(8,128)} custom-call(f32[160,128]{1,0:T(8,128)S(1)} %bitcast.7, f32[8,128]{1,0:T(8,128)S(1)} %get-tuple-element.39.own_ref, f32[384,128]{1,0:T(8,128)S(1)} %get-tuple-element.40.base_ref, f32[768,128]{1,0:T(8,128)S(1)} %get-tuple-element.41.down_ref, f32[512,256]{1,0:T(8,128)S(1)} %get-tuple-element.42.across_ref, ...), custom_call_target="tpu_custom_call" | custom-call | tf_op jit(solution)/shard_map/pallas_call | solution.py:381
Async XLA Ops:
  2.7 17.5 %all-to-all-start = ((f32[80,2,128]{2,1,0:T(2,128)}), f32[80,2,128]{2,1,0:T(2,128)S(1)}, u32[]{:S(2)}, u32[]{:S(2)}) async-start(f32[80,2,128]{2,1,0:T(2,128)} %bitcast), calls=%async_computation | async-start | bytes 163840 | tf_op jit(solution)/shard_map/all_to_all | solution.py:392

commit v2 on v0

v2 whole, which is shorter than its diff:
```python
import jax
import jax.numpy as jnp
import numpy as np
from jax import lax
from jax.experimental import pallas as pl
from jax.experimental.pallas import tpu as pltpu
from jax.sharding import Mesh, PartitionSpec as P

F32 = jnp.float32
BF16 = jnp.bfloat16
EXACT = lax.Precision.HIGHEST
NY, NZ = 1536, 8192
WALLS, STRIPS = 8, 64
PAIRS, PEERS = STRIPS // 2, 2 * WALLS
ROWS, COLS = NY // WALLS, NZ // STRIPS
GROUP = 4
OWNED = NY // PEERS
TILES = GROUP * OWNED // COLS
CHUNK = 10
SINE_Z, ENDS, EDGES, PICK, BOX_ROWS = 384, 512, 528, 544, 560
GHOST, MU_ROW, MU_COL, CLASS_ROWS = 0, 24, 48, 432
PHI, LAM_ROW, ENDS_Z, MU_BOX, SHARED_ROWS = 128, 136, 144, 152, 152


def halves(table):
    high = table.astype(np.float32).astype(BF16).astype(np.float64)
    return high, table - high


def sine_table(n):
    i = np.arange(1, n + 1)
    return np.sqrt(2 / (n + 1)) * np.sin(np.pi * np.outer(i, i) / (n + 1)), 4 * np.sin(np.pi * i / (2 * (n + 1))) ** 2


def tables():
    sine_y, mu_box = sine_table(ROWS)
    sine_z, lam = sine_table(COLS)
    ends_y, ends_z = sine_y[[0, -1]], sine_z[[0, -1]]
    boxes = np.zeros((BOX_ROWS, 256))
    boxes[:ROWS, :ROWS], boxes[ROWS:SINE_Z, :ROWS] = halves(sine_y)
    boxes[SINE_Z:ENDS, :COLS], boxes[SINE_Z:ENDS, COLS:] = halves(sine_z)
    boxes[ENDS : ENDS + 2, :ROWS], boxes[ENDS + 8 : ENDS + 10, :ROWS] = halves(ends_y)
    boxes[EDGES : EDGES + 2, :COLS], boxes[EDGES + 8 : EDGES + 10, :COLS] = halves(ends_z)
    boxes[PICK, 0], boxes[PICK + 1, COLS - 1] = -0.5, 0.5
    both = mu_box[:, None] + lam[None, :]
    shared = np.zeros((SHARED_ROWS, 256))
    shared[:PHI, :ROWS] = both.T
    shared[:PHI, ROWS:] = 1.0
    shared[PHI:LAM_ROW, :ROWS] = ends_y[0]
    shared[LAM_ROW:ENDS_Z, :COLS] = lam
    shared[ENDS_Z : ENDS_Z + 2, :COLS] = ends_z
    r, wall = np.arange(ROWS), np.arange(WALLS)
    known = np.zeros((GROUP, 4, CLASS_ROWS, COLS))
    mix = np.zeros((GROUP, 128, COLS))
    into = np.zeros((GROUP, 2 * GROUP * ROWS, 256))
    back = np.zeros((GROUP, 4, GROUP * OWNED, 4 * ROWS))
    for c in range(GROUP):
        fold = np.zeros((64, 64))
        for k in range(GROUP):
            mode = c + 4 * k + PEERS * np.arange(OWNED)
            norm = np.where(mode == 0, np.sqrt(1 / NY), np.sqrt(2 / NY))
            angle = np.pi * np.outer(2 * r + 1, mode) / (2 * NY)
            turn = np.pi * (c + 4 * k) * wall / 8
            for n, wave in enumerate((np.cos(angle), np.sin(angle))):
                rows = slice(ROWS * (2 * k + n), ROWS * (2 * k + n + 1))
                into[c, rows, :OWNED], into[c, rows, COLS : COLS + OWNED] = halves(sine_y @ (norm * wave))
            for line in range(4):
                for core in range(2):
                    box = 16 * line + 8 * core + wall
                    fold[16 * k + 2 * line + core, box] = np.cos(turn)
                    fold[16 * k + 8 + 2 * line + core, box] = -np.sin(turn)
        mix[c, :64, :64], mix[c, 64:, :64] = halves(fold)
        mode = (c + 4 * np.arange(GROUP)[:, None] + PEERS * np.arange(OWNED)[None, :]).reshape(-1)
        norm = np.where(mode == 0, np.sqrt(1 / NY), np.sqrt(2 / NY))
        mu = 4 * np.sin(np.pi * mode / (2 * NY)) ** 2
        for high in range(4):
            for low in range(2):
                w = 2 * high + low
                table = norm[:, None] * np.cos(np.pi * np.outer(mode, 2 * (ROWS * w + r) + 1) / (2 * NY)) @ sine_y
                here, other = slice(ROWS * low, ROWS * (low + 1)), slice(ROWS * (2 + low), ROWS * (3 + low))
                back[c, high, :, here], back[c, high, :, other] = halves(table)
                for g in range(2):
                    y = ROWS * (w + g) + g - 1
                    row = (norm * np.cos(np.pi * mode * (2 * y + 1) / (2 * NY))).reshape(TILES, COLS)
                    for core in range(2):
                        known[c, high, 4 * g + 2 * core + low : MU_ROW : 8] = row
            known[c, high, MU_ROW:MU_COL] = np.concatenate([np.repeat(mu.reshape(TILES, COLS), 4, 0)] * 2)
            known[c, high, MU_COL:] = mu[:, None]
    whole = dict(both=both, shared=shared, known=known)
    half = dict(boxes=boxes, mix=mix, into=into, back=back)
    return {k: np.asarray(v, np.float32) for k, v in whole.items()}, {k: np.asarray(v, np.float32) for k, v in half.items()}


def dot(a, b, dims):
    return lax.dot_general(a, b, (dims, ((), ())), precision=EXACT, preferred_element_type=F32)


def fast(a, b, dims=((1,), (0,))):
    return lax.dot_general(a, b, (dims, ((), ())), preferred_element_type=F32)


def ids(shape, dim):
    return lax.broadcasted_iota(jnp.int32, shape, dim)


def pieces(value):
    high = value.astype(BF16).astype(F32)
    return high, value - high


def parts(value):
    return [piece.astype(BF16) for piece in pieces(value)]


def stacked(value):
    return jnp.concatenate(pieces(value), 0).astype(BF16)


def beside(value):
    return jnp.concatenate(parts(value), 1)


def joined(product, rows, width=COLS, at=0):
    here, other = slice(at, at + width), slice(at + width, at + 2 * width)
    return product[:rows, here] + (product[:rows, other] + product[rows:, here])


def start(pairs, sems):
    copies = [pltpu.make_async_copy(*pair, sems.at[i]) for i, pair in enumerate(pairs)]
    for copy in copies:
        copy.start()
    return copies


def pack(lines):
    tails = [jnp.concatenate([lines[side][:, COLS:ROWS], lines[2 + side][:, COLS:ROWS]], 1) for side in range(2)]
    return [line[:, :COLS] for line in lines] + tails


def unpack(rows):
    return [
        jnp.concatenate([rows[2 * plane + side], rows[4 + side][:, 64 * plane : 64 * plane + 64]], 1)
        for plane in range(2) for side in range(2)
    ]


def box_kernel(
    wave_hbm, vel_hbm, both_hbm, boxes_hbm,
    out_ref, freq_ref, solve_ref, boxes_ref,
    wave_ref, vel_ref, both_ref, sems,
):
    copies = start([
        (wave_hbm, wave_ref), (both_hbm, both_ref), (vel_hbm.at[:, 0], vel_ref.at[:, 0]),
        (vel_hbm.at[:, 1], vel_ref.at[:, 1]), (boxes_hbm, boxes_ref),
    ], sems)
    row, lane = ids((ROWS, COLS), 0), ids((ROWS, COLS), 1)
    wall = 2 * lax.axis_index("high") + lax.axis_index("low")
    low = jnp.where(wall > 0, -0.5, 0.0)
    high = jnp.where(wall < WALLS - 1, 0.5, 0.0)
    copies[0].wait()
    copies[1].wait()
    for plane in range(2):
        wave = wave_ref[plane]
        solve_ref[ROWS * plane : ROWS * (plane + 1), :] = -1.0 / (wave * wave + both_ref[...])
    sources, rims, sides = [], [], []
    for plane in range(2):
        copies[2 + plane].wait()
        u, v, w = (vel_ref[c, plane] for c in range(3))
        above = jnp.where(row == ROWS - 1, 0.0, pltpu.roll(v, ROWS - 1, 0))
        below = jnp.where(row == 0, 0.0, pltpu.roll(v, 1, 0))
        after = jnp.where(lane == COLS - 1, 0.0, pltpu.roll(w, COLS - 1, 1))
        before = jnp.where(lane == 0, 0.0, pltpu.roll(w, 1, 1))
        sources += parts(wave_ref[plane] * u + 0.5 * ((above - below) + (after - before)))
        rims += [low * v[0:1], high * v[ROWS - 1 :]]
        sides.append(parts(w))
    copies[4].wait()
    sine, sine_z = boxes_ref[:SINE_Z, :ROWS], boxes_ref[SINE_Z:ENDS, :]
    product = fast(sine, jnp.concatenate(sources, 1))
    product = fast(jnp.concatenate([stacked(joined(product, ROWS, at=256 * p)) for p in range(2)], 0), sine_z)
    insides = []
    for plane in range(2):
        freq = joined(product[2 * ROWS * plane : 2 * ROWS * (plane + 1)], ROWS)
        rows = slice(ROWS * plane, ROWS * (plane + 1))
        freq_ref[rows, :] = freq
        insides.append(parts(freq * solve_ref[rows, :]))
    pick, edge = boxes_ref[PICK:BOX_ROWS, :COLS], boxes_ref[EDGES:PICK, :COLS]
    across = ((1,), (1,))
    halo = [(fast(pick, high, across) + fast(pick, low, across))[0:2] for high, low in sides]
    halo = stacked(jnp.concatenate(halo + [jnp.zeros((4, ROWS), F32)], 0))
    left, right = fast(halo, boxes_ref[:ROWS, :]), fast(halo, boxes_ref[ROWS:SINE_Z, :])
    halo = (left[0:8] + (left[8:16] + right[0:8]))[:, :ROWS]
    lines = []
    for plane, (high, low) in enumerate(insides):
        left, right = fast(edge, high, across), fast(edge, low, across)
        line = left[0:2] + (left[8:10] + right[0:2]) + halo[2 * plane : 2 * plane + 2]
        lines += [line[0:1], line[1:2]]
    ends = fast(boxes_ref[ENDS:EDGES, :ROWS], jnp.concatenate(insides[0] + insides[1], 1))
    ends = [joined(ends, 8, at=256 * p)[0:2] for p in range(2)]
    rims = fast(stacked(jnp.concatenate(rims + [jnp.zeros((4, COLS), F32)], 0)), sine_z)
    ends = jnp.concatenate(ends, 0) + joined(rims, 8)[0:4]
    four = jnp.concatenate((pack(lines) + [ends]) * 4, 0)
    for group in range(PEERS // 4):
        out_ref[4 * CHUNK * group : 4 * CHUNK * (group + 1), :] = four


def decay(shift):
    root = jnp.sqrt(shift * (shift + 4.0))
    delta = (shift + root) / (2.0 + shift + root)
    return 1.0 - delta, delta * (2.0 - delta), -jnp.log1p(-delta)


def factor_kernel(
    wave_hbm, shared_hbm, known_hbm, mix_hbm, into_hbm, back_hbm,
    chain_ref, reach_ref, cauchy_ref, ring_ref, pair_ref, rims_ref, mix_ref, into_ref, back_ref,
    wave_ref, shared_ref, known_ref, sems,
):
    pair, high = lax.axis_index("pair"), lax.axis_index("high")
    mine = 2 * lax.axis_index("core") + lax.axis_index("low")
    copies = start([
        (wave_hbm, wave_ref), (shared_hbm, shared_ref), (known_hbm.at[mine, high], known_ref), (mix_hbm.at[mine], mix_ref),
        (into_hbm.at[mine], into_ref), (back_hbm.at[mine, high], back_ref),
    ], sems)
    for copy in copies[:3]:
        copy.wait()
    waves = [wave_ref[p] * wave_ref[p] for p in range(2)]
    row = ids((8, COLS), 0)
    lam = shared_ref[LAM_ROW:ENDS_Z, :COLS]
    for p in range(2):
        at = COLS * p
        reach_ref[at : at + COLS, :] = beside(shared_ref[PHI : PHI + 1, :] / (waves[p] + shared_ref[:PHI, :]))
        rows = slice(GROUP * OWNED * p, GROUP * OWNED * (p + 1))
        cauchy_ref[rows, :] = beside(1.0 / (known_ref[MU_COL:, :] + (waves[p] + lam[0:1])))
        rho, gap, theta = decay(waves[p] + lam)
        step = -1.0 * ROWS * theta
        scale = 1.0 / (gap * (1.0 - jnp.exp(-2.0 * NY * theta)))
        cross = jnp.exp(-(ROWS + 1.0) * theta)

        def reach(n):
            return jnp.exp(step * lax.bitwise_and(n, 15).astype(F32))

        for other in range(WALLS):
            up, down = reach(row - 1 - other) + rho * reach(15 - row - other), reach(row + other) + rho * reach(other - row)
            at = 32 * (WALLS * p + other)
            chain_ref[at : at + 8, :] = scale * (cross * up + down)
            chain_ref[at + 8 : at + 16, :] = scale * (up + cross * down)
            up, down = rho * reach(row - other) + reach(14 - row - other), rho * reach(row + 1 + other) + reach(other - row - 1)
            chain_ref[at + 16 : at + 24, :] = scale * (cross * up + down)
            chain_ref[at + 24 : at + 32, :] = scale * (up + cross * down)
    place = ids((24, COLS), 0)
    second, leftward = place % 4 >= 2, place % 2 == 0
    mu = known_ref[MU_ROW:MU_COL, :]
    _, _, theta = decay(jnp.where(second, waves[1], waves[0]) + mu)
    step = -2.0 * COLS * theta
    for group in range(PAIRS // 2):
        other = 2 * group + place // 12
        n = lax.bitwise_and(jnp.where(leftward, other - pair - 1, pair - 1 - other), PAIRS - 1)
        ring_ref[24 * group : 24 * group + 24, :] = jnp.exp(step * n.astype(F32))
    coefs = [[], [], [], []]
    for tile in range(TILES):
        rho, gap, theta = decay(jnp.where(row >= 4, waves[1], waves[0]) + mu[4 * tile : 4 * tile + 1])
        block = jnp.exp(-1.0 * COLS * theta)
        pair_ref[8 * tile : 8 * tile + 8, :] = jnp.exp(-(COLS + 1.0) * theta)
        pair_ref[24 + 8 * tile : 32 + 8 * tile, :] = block
        period = 1.0 - jnp.exp(-1.0 * NZ * theta)
        for i, value in enumerate((rho, 1.0 / (gap * period), period, block)):
            coefs[i] += [value[0:1], value[4:5]]
    for i in range(4):
        pair_ref[48 + 8 * i : 56 + 8 * i, :] = jnp.concatenate(coefs[i] + coefs[i][:2], 0)
    rims_ref[0:24, :] = known_ref[GHOST:MU_ROW, :]
    rims_ref[24:32, :] = shared_ref[ENDS_Z:MU_BOX, :COLS]
    for copy in copies[3:]:
        copy.wait()


def strip_kernel(in_ref, chain_ref, reach_ref, pair_ref, rims_ref, mix_ref, into_ref, out_ref, own_ref, sums_ref, near_ref):
    box = [in_ref[pl.ds(i, PEERS, stride=CHUNK), :] for i in range(6)]
    ends = rims_ref[24:26, :]
    lines = unpack(box)
    even = ids((2 * PEERS, ROWS), 1) % 2 == 0
    added = []
    for plane in range(2):
        tops, bottoms = [], []
        for core in range(2):
            top = bottom = None
            for other in range(WALLS):
                at = 32 * (WALLS * plane + other)
                source = CHUNK * (WALLS * core + other) + 6 + 2 * plane
                first, last = in_ref[source : source + 1, :], in_ref[source + 1 : source + 2, :]
                weight = [chain_ref[at + 8 * i : at + 8 * i + 8, :] for i in range(4)]
                one, two = weight[0] * first + weight[1] * last, weight[2] * first + weight[3] * last
                top, bottom = (one, two) if top is None else (top + one, bottom + two)
            tops.append(top)
            bottoms.append(bottom)
        top, bottom = jnp.concatenate(tops, 0), jnp.concatenate(bottoms, 0)
        near_ref[pl.ds(2 * plane, PEERS, stride=8), :] = top
        near_ref[pl.ds(2 * plane + 1, PEERS, stride=8), :] = bottom
        sums = [value * ends[side : side + 1] for value in (top + bottom, top - bottom) for side in range(2)]
        product = fast(stacked(jnp.concatenate(sums, 0)), reach_ref[COLS * plane : COLS * (plane + 1), :])
        product = joined(product, 4 * PEERS, 256)[:, :ROWS]
        added.append(jnp.where(even, product[: 2 * PEERS], product[2 * PEERS :]))
    mine = 8 * lax.axis_index("core") + 2 * lax.axis_index("high") + lax.axis_index("low")
    own_ref[...] = near_ref[pl.ds(pl.multiple_of(8 * mine, 8), 8), :]
    lines = jnp.concatenate(lines, 0) + jnp.concatenate(added, 0)
    lines = jnp.concatenate([lines, jnp.zeros((4 * PEERS, 256 - ROWS), F32)], 1)
    folded = joined(fast(mix_ref[:, :64], beside(lines)), 64, 256)
    modes = []
    for k in range(GROUP):
        both = jnp.concatenate([folded[16 * k : 16 * k + 8, :ROWS], folded[16 * k + 8 : 16 * k + 16, :ROWS]], 1)
        modes.append(joined(fast(stacked(both), into_ref[2 * ROWS * k : 2 * ROWS * (k + 1), :]), 8))
    modes = [modes[0]] + [pltpu.roll(modes[k], COLS - 32 * k, 1) for k in range(1, GROUP)]
    row, lane = ids((8, COLS), 0), ids((8, COLS), 1)
    out = []
    for tile in range(TILES):
        value = jnp.where(lane < 96 - 32 * tile, modes[tile], modes[tile + 1])
        at = 8 * tile
        near = jnp.where(row % 4 < 2, pltpu.roll(value, 6, 0), pltpu.roll(value, 2, 0))
        value = value + pair_ref[at : at + 8, :] * near
        sums_ref[at : at + 8, :] = value
        near = jnp.where(row % 2 == 0, pltpu.roll(value, 7, 0), pltpu.roll(value, 1, 0))
        value = value + pair_ref[24 + at : 32 + at, :] * near
        out += [value[0:1], value[3:5], value[7:8]]
    out = jnp.concatenate(out * 2, 0)
    for group in range(PAIRS // 2):
        out_ref[24 * group : 24 * group + 24, :] = out


def ring_kernel(in_ref, sums_ref, ring_ref, pair_ref, rims_ref, back_ref, cauchy_ref, out_ref, far_ref, line_ref):
    total = in_ref[0:24, :] * ring_ref[0:24, :]
    for group in range(1, PAIRS // 2):
        total = total + in_ref[24 * group : 24 * group + 24, :] * ring_ref[24 * group : 24 * group + 24, :]
    far_ref[...] = total
    count = 2 * TILES
    after, before = (
        far_ref[pl.ds(i, count, stride=2), :] + far_ref[pl.ds(12 + i, count, stride=2), :] for i in range(2)
    )
    rho, scale, period, block = (pair_ref[48 + 8 * i : 48 + 8 * i + count, :] for i in range(4))
    left0, left1, right0, right1 = (period * sums_ref[pl.ds(i, count, stride=4), :] for i in range(4))
    coming, going = block * before + right0, block * after + left1
    ghosts = (
        scale * (before + rho * (left0 + block * going)), scale * (coming + rho * going),
        scale * (rho * coming + going), scale * (rho * (right1 + block * coming) + after),
    )
    for i, value in enumerate(ghosts):
        line_ref[pl.ds(i, count, stride=4), :] = value
    tiles = [line_ref[8 * tile : 8 * tile + 8, :] for tile in range(TILES)]
    cells = joined(fast(stacked(jnp.concatenate(tiles, 1)), back_ref[...]), 8, 2 * ROWS)
    ends = rims_ref[24:26, :]
    is_first = ids((8, COLS), 0) % 4 < 2
    rims = []
    for plane in range(2):
        both = []
        for side in range(2):
            at = 4 * plane + 2 * side
            lines = [jnp.where(is_first, tile[at : at + 1], tile[at + 1 : at + 2]) for tile in tiles]
            both.append(jnp.concatenate([rims_ref[8 * i : 8 * i + 8, :] * line for i, line in enumerate(lines)], 1))
        rows = slice(GROUP * OWNED * plane, GROUP * OWNED * (plane + 1))
        product = joined(fast(stacked(jnp.concatenate(both, 0)), cauchy_ref[rows, :]), 16)
        rims.append(product[:8] * ends[0:1] + product[8:] * ends[1:2])
    out = []
    for core in range(2):
        for low in range(2):
            at = 2 * core + low
            out += pack([cells[2 * i + core : 2 * i + core + 1, ROWS * low : ROWS * (low + 1)] for i in range(4)])
            out += [rims[plane][4 * g + at : 4 * g + at + 1] for plane in range(2) for g in range(2)]
    out_ref[...] = jnp.concatenate(out, 0)


def final_kernel(in_ref, own_ref, freq_ref, solve_ref, boxes_ref, out_hbm, out_ref, sems):
    total = (in_ref[0:CHUNK, :] + in_ref[CHUNK : 2 * CHUNK, :]) + (in_ref[2 * CHUNK : 3 * CHUNK, :] + in_ref[3 * CHUNK :, :])
    sides = unpack([total[i : i + 1] for i in range(6)])
    rims = total[6:10] + own_ref[0:4, :]
    sine, sine_z = boxes_ref[:SINE_Z, :ROWS], boxes_ref[SINE_Z:ENDS, :]
    ends_y, ends_z = boxes_ref[ENDS:EDGES, :ROWS].astype(F32), boxes_ref[EDGES:PICK, :COLS].astype(F32)
    ends_y, ends_z = ends_y[0:2] + ends_y[8:10], ends_z[0:2] + ends_z[8:10]
    freqs = []
    for plane in range(2):
        rows = slice(ROWS * plane, ROWS * (plane + 1))
        lhs = pieces(jnp.concatenate([ends_y] + sides[2 * plane : 2 * plane + 2] + [jnp.zeros((4, ROWS), F32)], 0))
        rhs = pieces(jnp.concatenate([rims[2 * plane : 2 * plane + 2], ends_z, jnp.zeros((4, COLS), F32)], 0))
        lhs = jnp.concatenate([lhs[0], lhs[0], lhs[1], lhs[1]], 0).astype(BF16)
        rhs = jnp.concatenate([rhs[0], rhs[1], rhs[0], rhs[1]], 0).astype(BF16)
        freqs.append(stacked((freq_ref[rows, :] - fast(lhs, rhs, ((0,), (0,)))) * solve_ref[rows, :]))
    product = fast(jnp.concatenate(freqs, 0), sine_z)
    lines = [beside(joined(product[2 * ROWS * p : 2 * ROWS * (p + 1)], ROWS)) for p in range(2)]
    product = fast(sine, jnp.concatenate(lines, 1))
    copies = []
    for plane in range(2):
        out_ref[plane] = joined(product, ROWS, at=256 * plane)
        copies += start([(out_ref.at[plane], out_hbm.at[plane])], sems.at[pl.ds(plane, 1)])
    for copy in copies:
        copy.wait()


VMEM = pl.BlockSpec(memory_space=pltpu.VMEM)
HBM = pl.BlockSpec(memory_space=pltpu.HBM)


def call(kernel, shapes, specs, *operands, scratch=(), into=VMEM):
    outs = [jax.ShapeDtypeStruct(s[0], s[1]) if isinstance(s[0], tuple) else jax.ShapeDtypeStruct(s, F32) for s in shapes]
    operands = [pltpu.with_memory_space_constraint(x, pltpu.HBM) if s is HBM else x for s, x in zip(specs, operands)]
    return pl.pallas_call(
        kernel,
        out_shape=outs if len(outs) > 1 else outs[0],
        in_specs=specs,
        out_specs=[into] * len(outs) if len(outs) > 1 else into,
        scratch_shapes=list(scratch),
        compiler_params=pltpu.CompilerParams(vmem_limit_bytes=24 << 20),
    )(*operands)


def exchange(block, axes):
    return lax.all_to_all(block, axes, split_axis=0, concat_axis=0, tiled=True)


def on_device(velocity, wave_x):
    whole, half = tables()
    t = {k: jnp.asarray(v) for k, v in whole.items()} | {k: jnp.asarray(v, BF16) for k, v in half.items()}
    pltpu_smem = pltpu.SMEM((2,), F32)
    sent, freq, solve, boxes = call(
        box_kernel, [(PEERS * CHUNK, COLS), (2 * ROWS, COLS), (2 * ROWS, COLS), ((BOX_ROWS, 256), BF16)],
        [HBM] * 4, wave_x, velocity, t["both"], t["boxes"],
        scratch=[
            pltpu_smem, pltpu.VMEM((3, 2, ROWS, COLS), F32), pltpu.VMEM((ROWS, COLS), F32),
            pltpu.SemaphoreType.DMA((5,)),
        ],
    )
    chain, reach, cauchy, ring, pair, rims, mix, into, back = call(
        factor_kernel,
        [
            (64 * WALLS, COLS), ((2 * COLS, 512), BF16), ((2 * GROUP * OWNED, 256), BF16), (12 * PAIRS, COLS), (80, COLS),
            (32, COLS), ((128, COLS), BF16), ((2 * GROUP * ROWS, 256), BF16), ((GROUP * OWNED, 4 * ROWS), BF16),
        ],
        [HBM] * 6, wave_x, t["shared"], t["known"], t["mix"], t["into"], t["back"],
        scratch=[pltpu_smem, pltpu.VMEM((SHARED_ROWS, 256), F32), pltpu.VMEM((CLASS_ROWS, COLS), F32), pltpu.SemaphoreType.DMA((6,))],
    )
    sent = exchange(sent.reshape(PEERS * CHUNK // 2, 2, COLS), ("core", "high", "low")).reshape(PEERS * CHUNK, COLS)
    modes, own, sums = call(
        strip_kernel, [(12 * PAIRS, COLS), (8, COLS), (24, COLS)], [VMEM] * 7,
        sent, chain, reach, pair, rims, mix, into, scratch=[pltpu.VMEM((8 * PEERS, COLS), F32)],
    )
    modes = exchange(modes.reshape(6 * PAIRS, 2, COLS), "pair").reshape(12 * PAIRS, COLS)
    cells = call(
        ring_kernel, [(GROUP * CHUNK, COLS)], [VMEM] * 7, modes, sums, ring, pair, rims, back, cauchy,
        scratch=[pltpu.VMEM((24, COLS), F32)] * 2,
    )
    cells = exchange(cells.reshape(GROUP * CHUNK // 2, 2, COLS), ("core", "low")).reshape(GROUP * CHUNK, COLS)
    return call(
        final_kernel, [(2, ROWS, COLS)], [VMEM] * 5, cells, own, freq, solve, boxes,
        scratch=[pltpu.VMEM((2, ROWS, COLS), F32), pltpu.SemaphoreType.DMA((2,))], into=HBM,
    )


def solution(mesh):
    fine = Mesh(mesh.devices.reshape(PAIRS, 2, WALLS // 2, 2), ("pair", "core", "high", "low"))
    wall, span = ("high", "low"), ("pair", "core")
    return jax.shard_map(
        on_device, mesh=fine, in_specs=(P(None, None, wall, span), P()), out_specs=P(None, wall, span), check_vma=False
    )
```

time: 55.1 us -> 51.8 us (0.940)
  blocking collectives: 32.1 us -> 28.8 us
    all_to_all x2, blocking collectives: 32.1 us -> 28.8 us  [exchange(): return lax.all_to_all(block, axes, split_axis=0, concat_axis=0, tiled=True)]
  transfers between devices with their start and end apart: 1 -> 1, of which waited for: 1 -> 1; matrix products, arithmetic and copies ran while one was open for 0% -> 0% of each run, Pallas kernels for 2% -> 3%
where the time goes in v2:
time: 51.8 us; the launch traced here: 51.5 us
  blocking collectives  28.8 us (56%)
  starting transfers between devices  10.2 us (20%)
  Pallas kernels  6.73 us (13%)
  waiting for transfers between devices  5.68 us (11%)
    all_to_all x2, blocking collectives, exchange(): return lax.all_to_all(block, axes, split_axis=0, concat_axis=0, tiled=True)  28.8 us
    all_to_all x1, starting transfers between devices, exchange(): return lax.all_to_all(block, axes, split_axis=0, concat_axis=0, tiled=True)  10.2 us
    pallas_call x5, Pallas kernels, call(): pl.pallas_call(kernel, out_shape=outs if len(outs) > 1 else outs[0], in_s...  6.73 us
    all_to_all x1, waiting for transfers between devices, exchange(): return lax.all_to_all(block, axes, split_axis=0, concat_axis=0, tiled=True)  5.68 us
  transfers between devices with their start and end apart: 1, of which 1 were waited for; matrix products, arithmetic and copies ran while one was open for 0% of the time, Pallas kernels for 3%

profile of v2, /device:TPU:1, one launch (start us, length us, event | category | flops | bytes accessed | tf_op | source)
XLA Modules:
  0.0 51.5 jit_solution(13651054906187952973)
XLA Ops:
  0.0 2.7 %shard_map.91 = (f32[160,128]{1,0:T(8,128)}, f32[384,128]{1,0:T(8,128)S(1)}, f32[384,128]{1,0:T(8,128)S(1)}, bf16[560,256]{1,0:T(8,128)(2,1)S(1)}) custom-call(f32[2]{0:T(128)} %wave_hbm.3, f32[3,2,192,128]{3,2,1,0:T(8,128)} %vel_hbm.1, f32[192,128]{1,0:T(8,128)} %constant.14.clone.both_hbm, bf16[560,256]{1,0:T(8,128)(2,1)} %constant.17.clone.boxes_hbm), custom_call_target="tpu_custom_call" | custom-call | tf_op jit(solution)/shard_map/pallas_call | solution.py:401
  2.7 10.2 %all-to-all-start = ((f32[80,2,128]{2,1,0:T(2,128)}), f32[80,2,128]{2,1,0:T(2,128)S(1)}, u32[]{:S(2)}, u32[]{:S(2)}) async-start(f32[80,2,128]{2,1,0:T(2,128)} %bitcast), calls=%async_computation | async-start | bytes 163840 | tf_op jit(solution)/shard_map/all_to_all | solution.py:412
  12.9 1.6 %shard_map.92 = (f32[512,128]{1,0:T(8,128)S(1)}, bf16[256,512]{1,0:T(8,128)(2,1)S(1)}, bf16[768,256]{1,0:T(8,128)(2,1)S(1)}, f32[384,128]{1,0:T(8,128)S(1)}, f32...) custom-call(f32[2]{0:T(128)} %wave_hbm.3, ...), custom_call_target="tpu_custom_call" | custom-call | tf_op jit(solution)/shard_map/pallas_call | solution.py:401
  14.5 5.7 %all-to-all-done = f32[80,2,128]{2,1,0:T(2,128)S(1)} async-done(((f32[80,2,128]{2,1,0:T(2,128)}), f32[80,2,128]{2,1,0:T(2,128)S(1)}, u32[]{:S(2)}, u32[]{:S(2)}) %all-to-all-start) | async-done | bytes 81952 | tf_op jit(solution)/shard_map/all_to_all | solution.py:412
  20.2 0.8 %shard_map.93 = (f32[384,128]{1,0:T(8,128)S(1)}, f32[8,128]{1,0:T(8,128)S(1)}, f32[24,128]{1,0:T(8,128)S(1)}) custom-call(f32[160,128]{1,0:T(8,128)S(1)} %bitcast.7, f32[512,128]{1,0:T(8,128)S(1)} %get-tuple-element.22.chain_ref, bf16[256,512]{1,0:T(8,128)(2,1)S(1)} %get-tuple-element.23.reach_ref, f32[80,128]{1,0:T(8,128)S(1)} %get-tuple-element.24.pair_ref, ...), custom_call_target="tpu_custom_call" | custom-call | tf_op jit(solution)/shard_map/pallas_call | solution.py:401
  21.0 20.6 %all_to_all.15 = f32[192,2,128]{2,1,0:T(2,128)S(1)} all-to-all(f32[192,2,128]{2,1,0:T(2,128)S(1)} %bitcast.8), channel_id=1, replica_groups=mesh['pair'=32,'core'=2,'high'=4,'low'=2] {'pair'}, dimensions={0} | all-to-all | bytes 393216 | tf_op jit(solution)/shard_map/all_to_all | solution.py:412
  41.5 0.3 shard_map.94
  41.8 8.3 %all_to_all.16 = f32[20,2,128]{2,1,0:T(2,128)S(1)} all-to-all(f32[20,2,128]{2,1,0:T(2,128)S(1)} %bitcast.9), channel_id=1, replica_groups=mesh['pair'=32,'core'=2,'high'=4,'low'=2] {'core','low'}, dimensions={0} | all-to-all | bytes 40960 | tf_op jit(solution)/shard_map/all_to_all | solution.py:412
  50.1 1.4 %shard_map.95 = f32[2,192,128]{2,1,0:T(8,128)} custom-call(f32[40,128]{1,0:T(8,128)S(1)} %bitcast.10, f32[8,128]{1,0:T(8,128)S(1)} %get-tuple-element.33.own_ref, f32[384,128]{1,0:T(8,128)S(1)} %get-tuple-element.34.freq_ref, f32[384,128]{1,0:T(8,128)S(1)} %get-tuple-element.35.solve_ref, bf16[560,256]{1,0:T(8,128)(2,1)S(1)} %get-tuple-element.36.boxes_ref), custom_call_target="tpu_custom_call" | custom-call | tf_op jit(solution)/shard_map/pallas_call | solution.py:401
Async XLA Ops:
  2.7 17.5 %all-to-all-start = ((f32[80,2,128]{2,1,0:T(2,128)}), f32[80,2,128]{2,1,0:T(2,128)S(1)}, u32[]{:S(2)}, u32[]{:S(2)}) async-start(f32[80,2,128]{2,1,0:T(2,128)} %bitcast), calls=%async_computation | async-start | bytes 163840 | tf_op jit(solution)/shard_map/all_to_all | solution.py:412

commit v3 on v2

--- a/solution.py
+++ b/solution.py
@@ -145,13 +145,17 @@
 
 
 def box_kernel(
-    wave_hbm, vel_hbm, both_hbm, boxes_hbm,
+    wave_hbm, vel_hbm, both_hbm, boxes_hbm, shared_hbm, known_hbm, mix_hbm, into_hbm, back_hbm,
     out_ref, freq_ref, solve_ref, boxes_ref,
-    wave_ref, vel_ref, both_ref, sems,
+    chain_ref, reach_ref, cauchy_ref, ring_ref, pair_ref, rims_ref, mix_ref, into_ref, back_ref,
+    wave_ref, vel_ref, both_ref, shared_ref, known_ref, sems,
 ):
+    mine, high = 2 * lax.axis_index("core") + lax.axis_index("low"), lax.axis_index("high")
     copies = start([
         (wave_hbm, wave_ref), (both_hbm, both_ref), (vel_hbm.at[:, 0], vel_ref.at[:, 0]),
-        (vel_hbm.at[:, 1], vel_ref.at[:, 1]), (boxes_hbm, boxes_ref),
+        (vel_hbm.at[:, 1], vel_ref.at[:, 1]), (boxes_hbm, boxes_ref), (shared_hbm, shared_ref),
+        (known_hbm.at[mine, high], known_ref), (mix_hbm.at[mine], mix_ref), (into_hbm.at[mine], into_ref),
+        (back_hbm.at[mine, high], back_ref),
     ], sems)
     row, lane = ids((ROWS, COLS), 0), ids((ROWS, COLS), 1)
     wall = 2 * lax.axis_index("high") + lax.axis_index("low")
@@ -173,7 +177,8 @@
         sources += parts(wave_ref[plane] * u + 0.5 * ((above - below) + (after - before)))
         rims += [low * v[0:1], high * v[ROWS - 1 :]]
         sides.append(parts(w))
-    copies[4].wait()
+    for copy in copies[4:7]:
+        copy.wait()
     sine, sine_z = boxes_ref[:SINE_Z, :ROWS], boxes_ref[SINE_Z:ENDS, :]
     product = fast(sine, jnp.concatenate(sources, 1))
     product = fast(jnp.concatenate([stacked(joined(product, ROWS, at=256 * p)) for p in range(2)], 0), sine_z)
@@ -201,6 +206,9 @@
     four = jnp.concatenate((pack(lines) + [ends]) * 4, 0)
     for group in range(PEERS // 4):
         out_ref[4 * CHUNK * group : 4 * CHUNK * (group + 1), :] = four
+    factors(wave_ref, shared_ref, known_ref, chain_ref, reach_ref, cauchy_ref, ring_ref, pair_ref, rims_ref)
+    for copy in copies[7:]:
+        copy.wait()
 
 
 def decay(shift):
@@ -209,19 +217,10 @@
     return 1.0 - delta, delta * (2.0 - delta), -jnp.log1p(-delta)
 
 
-def factor_kernel(
-    wave_hbm, shared_hbm, known_hbm, mix_hbm, into_hbm, back_hbm,
-    chain_ref, reach_ref, cauchy_ref, ring_ref, pair_ref, rims_ref, mix_ref, into_ref, back_ref,
-    wave_ref, shared_ref, known_ref, sems,
+def factors(
+    wave_ref, shared_ref, known_ref, chain_ref, reach_ref, cauchy_ref, ring_ref, pair_ref, rims_ref,
 ):
-    pair, high = lax.axis_index("pair"), lax.axis_index("high")
-    mine = 2 * lax.axis_index("core") + lax.axis_index("low")
-    copies = start([
-        (wave_hbm, wave_ref), (shared_hbm, shared_ref), (known_hbm.at[mine, high], known_ref), (mix_hbm.at[mine], mix_ref),
-        (into_hbm.at[mine], into_ref), (back_hbm.at[mine, high], back_ref),
-    ], sems)
-    for copy in copies[:3]:
-        copy.wait()
+    pair = lax.axis_index("pair")
     waves = [wave_ref[p] * wave_ref[p] for p in range(2)]
     row = ids((8, COLS), 0)
     lam = shared_ref[LAM_ROW:ENDS_Z, :COLS]
@@ -268,8 +267,6 @@
         pair_ref[48 + 8 * i : 56 + 8 * i, :] = jnp.concatenate(coefs[i] + coefs[i][:2], 0)
     rims_ref[0:24, :] = known_ref[GHOST:MU_ROW, :]
     rims_ref[24:32, :] = shared_ref[ENDS_Z:MU_BOX, :COLS]
-    for copy in copies[3:]:
-        copy.wait()
 
 
 def strip_kernel(in_ref, chain_ref, reach_ref, pair_ref, rims_ref, mix_ref, into_ref, out_ref, own_ref, sums_ref, near_ref):
@@ -415,23 +412,19 @@
 def on_device(velocity, wave_x):
     whole, half = tables()
     t = {k: jnp.asarray(v) for k, v in whole.items()} | {k: jnp.asarray(v, BF16) for k, v in half.items()}
-    pltpu_smem = pltpu.SMEM((2,), F32)
-    sent, freq, solve, boxes = call(
-        box_kernel, [(PEERS * CHUNK, COLS), (2 * ROWS, COLS), (2 * ROWS, COLS), ((BOX_ROWS, 256), BF16)],
-        [HBM] * 4, wave_x, velocity, t["both"], t["boxes"],
-        scratch=[
-            pltpu_smem, pltpu.VMEM((3, 2, ROWS, COLS), F32), pltpu.VMEM((ROWS, COLS), F32),
-            pltpu.SemaphoreType.DMA((5,)),
-        ],
-    )
-    chain, reach, cauchy, ring, pair, rims, mix, into, back = call(
-        factor_kernel,
+    sent, freq, solve, boxes, chain, reach, cauchy, ring, pair, rims, mix, into, back = call(
+        box_kernel,
         [
+            (PEERS * CHUNK, COLS), (2 * ROWS, COLS), (2 * ROWS, COLS), ((BOX_ROWS, 256), BF16),
             (64 * WALLS, COLS), ((2 * COLS, 512), BF16), ((2 * GROUP * OWNED, 256), BF16), (12 * PAIRS, COLS), (80, COLS),
             (32, COLS), ((128, COLS), BF16), ((2 * GROUP * ROWS, 256), BF16), ((GROUP * OWNED, 4 * ROWS), BF16),
         ],
-        [HBM] * 6, wave_x, t["shared"], t["known"], t["mix"], t["into"], t["back"],
-        scratch=[pltpu_smem, pltpu.VMEM((SHARED_ROWS, 256), F32), pltpu.VMEM((CLASS_ROWS, COLS), F32), pltpu.SemaphoreType.DMA((6,))],
+        [HBM] * 9,
+        wave_x, velocity, t["both"], t["boxes"], t["shared"], t["known"], t["mix"], t["into"], t["back"],
+        scratch=[
+            pltpu.SMEM((2,), F32), pltpu.VMEM((3, 2, ROWS, COLS), F32), pltpu.VMEM((ROWS, COLS), F32),
+            pltpu.VMEM((SHARED_ROWS, 256), F32), pltpu.VMEM((CLASS_ROWS, COLS), F32), pltpu.SemaphoreType.DMA((10,)),
+        ],
     )
     sent = exchange(sent.reshape(PEERS * CHUNK // 2, 2, COLS), ("core", "high", "low")).reshape(PEERS * CHUNK, COLS)
     modes, own, sums = call(

time: 51.8 us -> 51.2 us (0.988)
  blocking collectives: 28.8 us -> 46.1 us
  starting transfers between devices: 10.2 us -> 0 us
  waiting for transfers between devices: 5.68 us -> 0 us
  Pallas kernels: 6.73 us -> 4.81 us
    all_to_all x2 -> x3, blocking collectives: 28.8 us -> 46.1 us  [exchange(): return lax.all_to_all(block, axes, split_axis=0, concat_axis=0, tiled=True)]
    all_to_all x1 -> x0, starting transfers between devices: 10.2 us -> none  [exchange(): return lax.all_to_all(block, axes, split_axis=0, concat_axis=0, tiled=True)]
    all_to_all x1 -> x0, waiting for transfers between devices: 5.68 us -> none  [exchange(): return lax.all_to_all(block, axes, split_axis=0, concat_axis=0, tiled=True)]
    pallas_call x5 -> x4, Pallas kernels: 6.73 us -> 4.81 us  [call(): pl.pallas_call(kernel, out_shape=outs if len(outs) > 1 else outs[0], in_s...]
  transfers between devices with their start and end apart: 1 -> 0, of which waited for: 1 -> 0; matrix products, arithmetic and copies ran while one was open for 0% -> 0% of each run, Pallas kernels for 3% -> 0%
where the time goes in v3:
time: 51.2 us; the launch traced here: 51 us
  blocking collectives  46.1 us (90%)
  Pallas kernels  4.81 us (9%)
    all_to_all x3, blocking collectives, exchange(): return lax.all_to_all(block, axes, split_axis=0, concat_axis=0, tiled=True)  46.1 us
    pallas_call x4, Pallas kernels, call(): pl.pallas_call(kernel, out_shape=outs if len(outs) > 1 else outs[0], in_s...  4.81 us

profile of v3, /device:TPU:1, one launch (start us, length us, event | category | flops | bytes accessed | tf_op | source)
XLA Modules:
  0.0 51.0 jit_solution(5589355845736635008)
XLA Ops:
  0.0 2.3 %shard_map.91 = (f32[160,128]{1,0:T(8,128)S(1)}, f32[384,128]{1,0:T(8,128)S(1)}, f32[384,128]{1,0:T(8,128)S(1)}, bf16[560,256]{1,0:T(8,128)(2,1)S(1)}, f32[512,1...) custom-call(f32[2]{0:T(128)} %wave_hbm.1, ...), custom_call_target="tpu_custom_call" | custom-call | tf_op jit(solution)/shard_map/pallas_call | solution.py:398
  2.3 16.6 %all_to_all.15 = f32[80,2,128]{2,1,0:T(2,128)S(1)} all-to-all(f32[80,2,128]{2,1,0:T(2,128)S(1)} %bitcast.9), channel_id=1, replica_groups=mesh['pair'=32,'core'=2,'high'=4,'low'=2] {'core','high','low'}, dimensions={0} | all-to-all | bytes 163840 | tf_op jit(solution)/shard_map/all_to_all | solution.py:409
  18.9 0.8 %shard_map.92 = (f32[384,128]{1,0:T(8,128)S(1)}, f32[8,128]{1,0:T(8,128)S(1)}, f32[24,128]{1,0:T(8,128)S(1)}) custom-call(f32[160,128]{1,0:T(8,128)S(1)} %bitcast.7, f32[512,128]{1,0:T(8,128)S(1)} %get-tuple-element.22.chain_ref, bf16[256,512]{1,0:T(8,128)(2,1)S(1)} %get-tuple-element.23.reach_ref, f32[80,128]{1,0:T(8,128)S(1)} %get-tuple-element.24.pair_ref, ...), custom_call_target="tpu_custom_call" | custom-call | tf_op jit(solution)/shard_map/pallas_call | solution.py:398
  19.7 21.2 %all_to_all.16 = f32[192,2,128]{2,1,0:T(2,128)S(1)} all-to-all(f32[192,2,128]{2,1,0:T(2,128)S(1)} %bitcast.8), channel_id=1, replica_groups=mesh['pair'=32,'core'=2,'high'=4,'low'=2] {'pair'}, dimensions={0} | all-to-all | bytes 393216 | tf_op jit(solution)/shard_map/all_to_all | solution.py:409
  40.9 0.3 shard_map.93
  41.3 8.3 %all_to_all.17 = f32[20,2,128]{2,1,0:T(2,128)S(1)} all-to-all(f32[20,2,128]{2,1,0:T(2,128)S(1)} %bitcast.10), channel_id=1, replica_groups=mesh['pair'=32,'core'=2,'high'=4,'low'=2] {'core','low'}, dimensions={0} | all-to-all | bytes 40960 | tf_op jit(solution)/shard_map/all_to_all | solution.py:409
  49.6 1.4 %shard_map.94 = f32[2,192,128]{2,1,0:T(8,128)} custom-call(f32[40,128]{1,0:T(8,128)S(1)} %bitcast.11, f32[8,128]{1,0:T(8,128)S(1)} %get-tuple-element.33.own_ref, f32[384,128]{1,0:T(8,128)S(1)} %get-tuple-element.34.freq_ref, f32[384,128]{1,0:T(8,128)S(1)} %get-tuple-element.35.solve_ref, bf16[560,256]{1,0:T(8,128)(2,1)S(1)} %get-tuple-element.36.boxes_ref), custom_call_target="tpu_custom_call" | custom-call | tf_op jit(solution)/shard_map/pallas_call | solution.py:398

commit v4 on v3

--- a/solution.py
+++ b/solution.py
@@ -12,12 +12,13 @@
 NY, NZ = 1536, 8192
 WALLS, STRIPS = 8, 64
 PAIRS, PEERS = STRIPS // 2, 2 * WALLS
+FIRST, FIRST_WALL = 23, 4
 ROWS, COLS = NY // WALLS, NZ // STRIPS
 GROUP = 4
 OWNED = NY // PEERS
 TILES = GROUP * OWNED // COLS
 CHUNK = 10
-SINE_Z, ENDS, EDGES, PICK, BOX_ROWS = 384, 512, 528, 544, 560
+SINE_Z, ENDS, EDGES, PICK, BOX_ROWS = 384, 640, 656, 672, 688
 GHOST, MU_ROW, MU_COL, CLASS_ROWS = 0, 24, 48, 432
 PHI, LAM_ROW, ENDS_Z, MU_BOX, SHARED_ROWS = 128, 136, 144, 152, 152
 
@@ -38,7 +39,8 @@
     ends_y, ends_z = sine_y[[0, -1]], sine_z[[0, -1]]
     boxes = np.zeros((BOX_ROWS, 256))
     boxes[:ROWS, :ROWS], boxes[ROWS:SINE_Z, :ROWS] = halves(sine_y)
-    boxes[SINE_Z:ENDS, :COLS], boxes[SINE_Z:ENDS, COLS:] = halves(sine_z)
+    boxes[SINE_Z : SINE_Z + COLS, :COLS], boxes[SINE_Z : SINE_Z + COLS, COLS:] = halves(sine_z)
+    boxes[SINE_Z + COLS : ENDS, :COLS] = boxes[SINE_Z : SINE_Z + COLS, :COLS]
     boxes[ENDS : ENDS + 2, :ROWS], boxes[ENDS + 8 : ENDS + 10, :ROWS] = halves(ends_y)
     boxes[EDGES : EDGES + 2, :COLS], boxes[EDGES + 8 : EDGES + 10, :COLS] = halves(ends_z)
     boxes[PICK, 0], boxes[PICK + 1, COLS - 1] = -0.5, 0.5
@@ -66,7 +68,7 @@
                 into[c, rows, :OWNED], into[c, rows, COLS : COLS + OWNED] = halves(sine_y @ (norm * wave))
             for line in range(4):
                 for core in range(2):
-                    box = 16 * line + 8 * core + wall
+                    box = 16 * line + 8 * core + (wall - FIRST_WALL) % WALLS
                     fold[16 * k + 2 * line + core, box] = np.cos(turn)
                     fold[16 * k + 8 + 2 * line + core, box] = -np.sin(turn)
         mix[c, :64, :64], mix[c, 64:, :64] = halves(fold)
@@ -120,6 +122,10 @@
     return jnp.concatenate(parts(value), 1)
 
 
+def summed(product):
+    return product[:, :COLS] + product[:, COLS:]
+
+
 def joined(product, rows, width=COLS, at=0):
     here, other = slice(at, at + width), slice(at + width, at + 2 * width)
     return product[:rows, here] + (product[:rows, other] + product[rows:, here])
@@ -179,7 +185,7 @@
         sides.append(parts(w))
     for copy in copies[4:7]:
         copy.wait()
-    sine, sine_z = boxes_ref[:SINE_Z, :ROWS], boxes_ref[SINE_Z:ENDS, :]
+    sine, sine_z = boxes_ref[:SINE_Z, :ROWS], boxes_ref[SINE_Z : SINE_Z + COLS, :]
     product = fast(sine, jnp.concatenate(sources, 1))
     product = fast(jnp.concatenate([stacked(joined(product, ROWS, at=256 * p)) for p in range(2)], 0), sine_z)
     insides = []
@@ -237,12 +243,16 @@
         def reach(n):
             return jnp.exp(step * lax.bitwise_and(n, 15).astype(F32))
 
-        for other in range(WALLS):
-            up, down = reach(row - 1 - other) + rho * reach(15 - row - other), reach(row + other) + rho * reach(other - row)
-            at = 32 * (WALLS * p + other)
+        here = lax.bitwise_and(row + FIRST_WALL, WALLS - 1)
+        for place in range(WALLS):
+            other = (place + FIRST_WALL) % WALLS
+            up = reach(here - 1 - other) + rho * reach(15 - here - other)
+            down = reach(here + other) + rho * reach(other - here)
+            at = 32 * (WALLS * p + place)
             chain_ref[at : at + 8, :] = scale * (cross * up + down)
             chain_ref[at + 8 : at + 16, :] = scale * (up + cross * down)
-            up, down = rho * reach(row - other) + reach(14 - row - other), rho * reach(row + 1 + other) + reach(other - row - 1)
+            up = rho * reach(here - other) + reach(14 - here - other)
+            down = rho * reach(here + 1 + other) + reach(other - here - 1)
             chain_ref[at + 16 : at + 24, :] = scale * (cross * up + down)
             chain_ref[at + 24 : at + 32, :] = scale * (up + cross * down)
     place = ids((24, COLS), 0)
@@ -251,7 +261,7 @@
     _, _, theta = decay(jnp.where(second, waves[1], waves[0]) + mu)
     step = -2.0 * COLS * theta
     for group in range(PAIRS // 2):
-        other = 2 * group + place // 12
+        other = FIRST + 2 * group + place // 12
         n = lax.bitwise_and(jnp.where(leftward, other - pair - 1, pair - 1 - other), PAIRS - 1)
         ring_ref[24 * group : 24 * group + 24, :] = jnp.exp(step * n.astype(F32))
     coefs = [[], [], [], []]
@@ -295,7 +305,8 @@
         product = fast(stacked(jnp.concatenate(sums, 0)), reach_ref[COLS * plane : COLS * (plane + 1), :])
         product = joined(product, 4 * PEERS, 256)[:, :ROWS]
         added.append(jnp.where(even, product[: 2 * PEERS], product[2 * PEERS :]))
-    mine = 8 * lax.axis_index("core") + 2 * lax.axis_index("high") + lax.axis_index("low")
+    wall = 2 * lax.axis_index("high") + lax.axis_index("low")
+    mine = 8 * lax.axis_index("core") + lax.bitwise_and(wall - FIRST_WALL, WALLS - 1)
     own_ref[...] = near_ref[pl.ds(pl.multiple_of(8 * mine, 8), 8), :]
     lines = jnp.concatenate(lines, 0) + jnp.concatenate(added, 0)
     lines = jnp.concatenate([lines, jnp.zeros((4 * PEERS, 256 - ROWS), F32)], 1)
@@ -316,6 +327,7 @@
         near = jnp.where(row % 2 == 0, pltpu.roll(value, 7, 0), pltpu.roll(value, 1, 0))
         value = value + pair_ref[24 + at : 32 + at, :] * near
         out += [value[0:1], value[3:5], value[7:8]]
+    sums_ref[24:32, :] = jnp.zeros((8, COLS), F32)
     out = jnp.concatenate(out * 2, 0)
     for group in range(PAIRS // 2):
         out_ref[24 * group : 24 * group + 24, :] = out
@@ -325,7 +337,8 @@
     total = in_ref[0:24, :] * ring_ref[0:24, :]
     for group in range(1, PAIRS // 2):
         total = total + in_ref[24 * group : 24 * group + 24, :] * ring_ref[24 * group : 24 * group + 24, :]
-    far_ref[...] = total
+    far_ref[0:24, :] = total
+    far_ref[24:32, :] = jnp.zeros((8, COLS), F32)
     count = 2 * TILES
     after, before = (
         far_ref[pl.ds(i, count, stride=2), :] + far_ref[pl.ds(12 + i, count, stride=2), :] for i in range(2)
@@ -376,9 +389,9 @@
         rhs = pieces(jnp.concatenate([rims[2 * plane : 2 * plane + 2], ends_z, jnp.zeros((4, COLS), F32)], 0))
         lhs = jnp.concatenate([lhs[0], lhs[0], lhs[1], lhs[1]], 0).astype(BF16)
         rhs = jnp.concatenate([rhs[0], rhs[1], rhs[0], rhs[1]], 0).astype(BF16)
-        freqs.append(stacked((freq_ref[rows, :] - fast(lhs, rhs, ((0,), (0,)))) * solve_ref[rows, :]))
-    product = fast(jnp.concatenate(freqs, 0), sine_z)
-    lines = [beside(joined(product[2 * ROWS * p : 2 * ROWS * (p + 1)], ROWS)) for p in range(2)]
+        freqs.append(beside((freq_ref[rows, :] - fast(lhs, rhs, ((0,), (0,)))) * solve_ref[rows, :]))
+    product = summed(fast(jnp.concatenate(freqs, 0), sine_z))
+    lines = [beside(product[ROWS * p : ROWS * (p + 1)]) for p in range(2)]
     product = fast(sine, jnp.concatenate(lines, 1))
     copies = []
     for plane in range(2):
@@ -405,8 +418,9 @@
     )(*operands)
 
 
-def exchange(block, axes):
-    return lax.all_to_all(block, axes, split_axis=0, concat_axis=0, tiled=True)
+def exchange(block, axes, order=None):
+    groups = None if order is None else [order]
+    return lax.all_to_all(block, axes, split_axis=0, concat_axis=0, tiled=True, axis_index_groups=groups)
 
 
 def on_device(velocity, wave_x):
@@ -426,15 +440,16 @@
             pltpu.VMEM((SHARED_ROWS, 256), F32), pltpu.VMEM((CLASS_ROWS, COLS), F32), pltpu.SemaphoreType.DMA((10,)),
         ],
     )
-    sent = exchange(sent.reshape(PEERS * CHUNK // 2, 2, COLS), ("core", "high", "low")).reshape(PEERS * CHUNK, COLS)
+    order = [WALLS * core + (FIRST_WALL + i) % WALLS for core in range(2) for i in range(WALLS)]
+    sent = exchange(sent.reshape(PEERS * CHUNK // 2, 2, COLS), ("core", "high", "low"), order).reshape(PEERS * CHUNK, COLS)
     modes, own, sums = call(
-        strip_kernel, [(12 * PAIRS, COLS), (8, COLS), (24, COLS)], [VMEM] * 7,
+        strip_kernel, [(12 * PAIRS, COLS), (8, COLS), (32, COLS)], [VMEM] * 7,
         sent, chain, reach, pair, rims, mix, into, scratch=[pltpu.VMEM((8 * PEERS, COLS), F32)],
     )
-    modes = exchange(modes.reshape(6 * PAIRS, 2, COLS), "pair").reshape(12 * PAIRS, COLS)
+    modes = exchange(modes.reshape(6 * PAIRS, 2, COLS), "pair", [(FIRST + i) % PAIRS for i in range(PAIRS)]).reshape(12 * PAIRS, COLS)
     cells = call(
         ring_kernel, [(GROUP * CHUNK, COLS)], [VMEM] * 7, modes, sums, ring, pair, rims, back, cauchy,
-        scratch=[pltpu.VMEM((24, COLS), F32)] * 2,
+        scratch=[pltpu.VMEM((32, COLS), F32)] * 2,
     )
     cells = exchange(cells.reshape(GROUP * CHUNK // 2, 2, COLS), ("core", "low")).reshape(GROUP * CHUNK, COLS)
     return call(

time: 51.2 us -> 45.6 us (0.89)
  blocking collectives: 46.1 us -> 40.6 us
    all_to_all x3, blocking collectives: 46.1 us -> 40.6 us  [exchange(): lax.all_to_all(block, axes, split_axis=0, concat_axis=0, tiled=True, axis...]
where the time goes in v4:
time: 45.6 us; the launch traced here: 45.3 us
  blocking collectives  40.6 us (89%)
  Pallas kernels  4.76 us (10%)
    all_to_all x3, blocking collectives, exchange(): lax.all_to_all(block, axes, split_axis=0, concat_axis=0, tiled=True, axis...  40.6 us
    pallas_call x4, Pallas kernels, call(): pl.pallas_call(kernel, out_shape=outs if len(outs) > 1 else outs[0], in_s...  4.76 us

profile of v4, /device:TPU:1, one launch (start us, length us, event | category | flops | bytes accessed | tf_op | source)
XLA Modules:
  0.0 45.3 jit_solution(16510734509233216445)
XLA Ops:
  0.0 2.4 %shard_map.91 = (f32[160,128]{1,0:T(8,128)S(1)}, f32[384,128]{1,0:T(8,128)S(1)}, f32[384,128]{1,0:T(8,128)S(1)}, bf16[688,256]{1,0:T(8,128)(2,1)S(1)}, f32[512,1...) custom-call(f32[2]{0:T(128)} %wave_hbm.1, ...), custom_call_target="tpu_custom_call" | custom-call | tf_op jit(solution)/shard_map/pallas_call | solution.py:411
  2.4 16.9 %all_to_all.15 = f32[80,2,128]{2,1,0:T(2,128)S(1)} all-to-all(f32[80,2,128]{2,1,0:T(2,128)S(1)} %bitcast.9), channel_id=1, replica_groups={{4,5,6,7,0,1,2,3,12,13,14,15,8,9,10,11},{20,21,22,23,16,17,18,19,28,29,..., dimensions={0} | all-to-all | bytes 163840 | tf_op jit(solution)/shard_map/all_to_all | solution.py:423
  19.2 0.8 %shard_map.92 = (f32[384,128]{1,0:T(8,128)S(1)}, f32[8,128]{1,0:T(8,128)S(1)}, f32[32,128]{1,0:T(8,128)S(1)}) custom-call(f32[160,128]{1,0:T(8,128)S(1)} %bitcast.7, f32[512,128]{1,0:T(8,128)S(1)} %get-tuple-element.22.chain_ref, bf16[256,512]{1,0:T(8,128)(2,1)S(1)} %get-tuple-element.23.reach_ref, f32[80,128]{1,0:T(8,128)S(1)} %get-tuple-element.24.pair_ref, ...), custom_call_target="tpu_custom_call" | custom-call | tf_op jit(solution)/shard_map/pallas_call | solution.py:411
  20.0 16.5 %all_to_all.16 = f32[192,2,128]{2,1,0:T(2,128)S(1)} all-to-all(f32[192,2,128]{2,1,0:T(2,128)S(1)} %bitcast.8), channel_id=1, replica_groups={{368,384,400,416,432,448,464,480,496,0,16,32,48,64,80,96,112,128,144,16..., dimensions={0} | all-to-all | bytes 393216 | tf_op jit(solution)/shard_map/all_to_all | solution.py:423
  36.5 0.3 shard_map.93
  36.9 7.2 %all_to_all.17 = f32[20,2,128]{2,1,0:T(2,128)S(1)} all-to-all(f32[20,2,128]{2,1,0:T(2,128)S(1)} %bitcast.10), channel_id=1, replica_groups=mesh['pair'=32,'core'=2,'high'=4,'low'=2] {'core','low'}, dimensions={0} | all-to-all | bytes 40960 | tf_op jit(solution)/shard_map/all_to_all | solution.py:423
  44.0 1.3 %shard_map.94 = f32[2,192,128]{2,1,0:T(8,128)} custom-call(f32[40,128]{1,0:T(8,128)S(1)} %bitcast.11, f32[8,128]{1,0:T(8,128)S(1)} %get-tuple-element.33.own_ref, f32[384,128]{1,0:T(8,128)S(1)} %get-tuple-element.34.freq_ref, f32[384,128]{1,0:T(8,128)S(1)} %get-tuple-element.35.solve_ref, bf16[688,256]{1,0:T(8,128)(2,1)S(1)} %get-tuple-element.36.boxes_ref), custom_call_target="tpu_custom_call" | custom-call | tf_op jit(solution)/shard_map/pallas_call | solution.py:411

commit v5 on v4

--- a/solution.py
+++ b/solution.py
@@ -68,7 +68,7 @@
                 into[c, rows, :OWNED], into[c, rows, COLS : COLS + OWNED] = halves(sine_y @ (norm * wave))
             for line in range(4):
                 for core in range(2):
-                    box = 16 * line + 8 * core + (wall - FIRST_WALL) % WALLS
+                    box = 16 * line + 8 * (1 - core) + (wall - FIRST_WALL) % WALLS
                     fold[16 * k + 2 * line + core, box] = np.cos(turn)
                     fold[16 * k + 8 + 2 * line + core, box] = -np.sin(turn)
         mix[c, :64, :64], mix[c, 64:, :64] = halves(fold)
@@ -306,7 +306,7 @@
         product = joined(product, 4 * PEERS, 256)[:, :ROWS]
         added.append(jnp.where(even, product[: 2 * PEERS], product[2 * PEERS :]))
     wall = 2 * lax.axis_index("high") + lax.axis_index("low")
-    mine = 8 * lax.axis_index("core") + lax.bitwise_and(wall - FIRST_WALL, WALLS - 1)
+    mine = 8 * (1 - lax.axis_index("core")) + lax.bitwise_and(wall - FIRST_WALL, WALLS - 1)
     own_ref[...] = near_ref[pl.ds(pl.multiple_of(8 * mine, 8), 8), :]
     lines = jnp.concatenate(lines, 0) + jnp.concatenate(added, 0)
     lines = jnp.concatenate([lines, jnp.zeros((4 * PEERS, 256 - ROWS), F32)], 1)
@@ -367,7 +367,7 @@
         product = joined(fast(stacked(jnp.concatenate(both, 0)), cauchy_ref[rows, :]), 16)
         rims.append(product[:8] * ends[0:1] + product[8:] * ends[1:2])
     out = []
-    for core in range(2):
+    for core in (1, 0):
         for low in range(2):
             at = 2 * core + low
             out += pack([cells[2 * i + core : 2 * i + core + 1, ROWS * low : ROWS * (low + 1)] for i in range(4)])
@@ -440,7 +440,8 @@
             pltpu.VMEM((SHARED_ROWS, 256), F32), pltpu.VMEM((CLASS_ROWS, COLS), F32), pltpu.SemaphoreType.DMA((10,)),
         ],
     )
-    order = [WALLS * core + (FIRST_WALL + i) % WALLS for core in range(2) for i in range(WALLS)]
+    near = [2 * core + low for core in (1, 0) for low in range(2)]
+    order = [WALLS * core + (FIRST_WALL + i) % WALLS for core in (1, 0) for i in range(WALLS)]
     sent = exchange(sent.reshape(PEERS * CHUNK // 2, 2, COLS), ("core", "high", "low"), order).reshape(PEERS * CHUNK, COLS)
     modes, own, sums = call(
         strip_kernel, [(12 * PAIRS, COLS), (8, COLS), (32, COLS)], [VMEM] * 7,
@@ -451,7 +452,7 @@
         ring_kernel, [(GROUP * CHUNK, COLS)], [VMEM] * 7, modes, sums, ring, pair, rims, back, cauchy,
         scratch=[pltpu.VMEM((32, COLS), F32)] * 2,
     )
-    cells = exchange(cells.reshape(GROUP * CHUNK // 2, 2, COLS), ("core", "low")).reshape(GROUP * CHUNK, COLS)
+    cells = exchange(cells.reshape(GROUP * CHUNK // 2, 2, COLS), ("core", "low"), near).reshape(GROUP * CHUNK, COLS)
     return call(
         final_kernel, [(2, ROWS, COLS)], [VMEM] * 5, cells, own, freq, solve, boxes,
         scratch=[pltpu.VMEM((2, ROWS, COLS), F32), pltpu.SemaphoreType.DMA((2,))], into=HBM,

time: 45.6 us -> 44.8 us (0.982)
  blocking collectives: 40.6 us -> 39.8 us
    all_to_all x3, blocking collectives: 40.6 us -> 39.8 us  [exchange(): lax.all_to_all(block, axes, split_axis=0, concat_axis=0, tiled=True, axis...]
where the time goes in v5:
time: 44.8 us; the launch traced here: 44.6 us
  blocking collectives  39.8 us (89%)
  Pallas kernels  4.76 us (11%)
    all_to_all x3, blocking collectives, exchange(): lax.all_to_all(block, axes, split_axis=0, concat_axis=0, tiled=True, axis...  39.8 us
    pallas_call x4, Pallas kernels, call(): pl.pallas_call(kernel, out_shape=outs if len(outs) > 1 else outs[0], in_s...  4.76 us

profile of v5, /device:TPU:1, one launch (start us, length us, event | category | flops | bytes accessed | tf_op | source)
XLA Modules:
  0.0 44.6 jit_solution(6744350093335995290)
XLA Ops:
  0.0 2.4 %shard_map.91 = (f32[160,128]{1,0:T(8,128)S(1)}, f32[384,128]{1,0:T(8,128)S(1)}, f32[384,128]{1,0:T(8,128)S(1)}, bf16[688,256]{1,0:T(8,128)(2,1)S(1)}, f32[512,1...) custom-call(f32[2]{0:T(128)} %wave_hbm.1, ...), custom_call_target="tpu_custom_call" | custom-call | tf_op jit(solution)/shard_map/pallas_call | solution.py:411
  2.4 16.5 %all_to_all.15 = f32[80,2,128]{2,1,0:T(2,128)S(1)} all-to-all(f32[80,2,128]{2,1,0:T(2,128)S(1)} %bitcast.9), channel_id=1, replica_groups={{12,13,14,15,8,9,10,11,4,5,6,7,0,1,2,3},{28,29,30,31,24,25,26,27,20,21,..., dimensions={0} | all-to-all | bytes 163840 | tf_op jit(solution)/shard_map/all_to_all | solution.py:423
  18.9 0.8 %shard_map.92 = (f32[384,128]{1,0:T(8,128)S(1)}, f32[8,128]{1,0:T(8,128)S(1)}, f32[32,128]{1,0:T(8,128)S(1)}) custom-call(f32[160,128]{1,0:T(8,128)S(1)} %bitcast.7, f32[512,128]{1,0:T(8,128)S(1)} %get-tuple-element.22.chain_ref, bf16[256,512]{1,0:T(8,128)(2,1)S(1)} %get-tuple-element.23.reach_ref, f32[80,128]{1,0:T(8,128)S(1)} %get-tuple-element.24.pair_ref, ...), custom_call_target="tpu_custom_call" | custom-call | tf_op jit(solution)/shard_map/pallas_call | solution.py:411
  19.7 16.3 %all_to_all.16 = f32[192,2,128]{2,1,0:T(2,128)S(1)} all-to-all(f32[192,2,128]{2,1,0:T(2,128)S(1)} %bitcast.8), channel_id=1, replica_groups={{368,384,400,416,432,448,464,480,496,0,16,32,48,64,80,96,112,128,144,16..., dimensions={0} | all-to-all | bytes 393216 | tf_op jit(solution)/shard_map/all_to_all | solution.py:423
  36.0 0.3 shard_map.93
  36.3 7.0 %all_to_all.17 = f32[20,2,128]{2,1,0:T(2,128)S(1)} all-to-all(f32[20,2,128]{2,1,0:T(2,128)S(1)} %bitcast.10), channel_id=1, replica_groups={{8,9,0,1},{10,11,2,3},{12,13,4,5},{14,15,6,7},{24,25,16,17},{26,27,18,1..., dimensions={0} | all-to-all | bytes 40960 | tf_op jit(solution)/shard_map/all_to_all | solution.py:423
  43.3 1.3 %shard_map.94 = f32[2,192,128]{2,1,0:T(8,128)} custom-call(f32[40,128]{1,0:T(8,128)S(1)} %bitcast.11, f32[8,128]{1,0:T(8,128)S(1)} %get-tuple-element.33.own_ref, f32[384,128]{1,0:T(8,128)S(1)} %get-tuple-element.34.freq_ref, f32[384,128]{1,0:T(8,128)S(1)} %get-tuple-element.35.solve_ref, bf16[688,256]{1,0:T(8,128)(2,1)S(1)} %get-tuple-element.36.boxes_ref), custom_call_target="tpu_custom_call" | custom-call | tf_op jit(solution)/shard_map/pallas_call | solution.py:411

commit v6 on v5

--- a/solution.py
+++ b/solution.py
@@ -12,7 +12,8 @@
 NY, NZ = 1536, 8192
 WALLS, STRIPS = 8, 64
 PAIRS, PEERS = STRIPS // 2, 2 * WALLS
-FIRST, FIRST_WALL = 23, 4
+WALL_ORDER = (4, 5, 3, 6, 2, 7, 1, 0)
+PAIR_ORDER = [8 * x + z for z in range(7, -1, -1) for x in (2, 3, 1, 0)]
 ROWS, COLS = NY // WALLS, NZ // STRIPS
 GROUP = 4
 OWNED = NY // PEERS
@@ -68,7 +69,7 @@
                 into[c, rows, :OWNED], into[c, rows, COLS : COLS + OWNED] = halves(sine_y @ (norm * wave))
             for line in range(4):
                 for core in range(2):
-                    box = 16 * line + 8 * (1 - core) + (wall - FIRST_WALL) % WALLS
+                    box = 16 * line + 8 * (1 - core) + np.argsort(WALL_ORDER)
                     fold[16 * k + 2 * line + core, box] = np.cos(turn)
                     fold[16 * k + 8 + 2 * line + core, box] = -np.sin(turn)
         mix[c, :64, :64], mix[c, 64:, :64] = halves(fold)
@@ -243,9 +244,9 @@
         def reach(n):
             return jnp.exp(step * lax.bitwise_and(n, 15).astype(F32))
 
-        here = lax.bitwise_and(row + FIRST_WALL, WALLS - 1)
+        here = sum(jnp.where(row == i, w, 0) for i, w in enumerate(WALL_ORDER))
         for place in range(WALLS):
-            other = (place + FIRST_WALL) % WALLS
+            other = WALL_ORDER[place]
             up = reach(here - 1 - other) + rho * reach(15 - here - other)
             down = reach(here + other) + rho * reach(other - here)
             at = 32 * (WALLS * p + place)
@@ -261,7 +262,7 @@
     _, _, theta = decay(jnp.where(second, waves[1], waves[0]) + mu)
     step = -2.0 * COLS * theta
     for group in range(PAIRS // 2):
-        other = FIRST + 2 * group + place // 12
+        other = jnp.where(place < 12, PAIR_ORDER[2 * group], PAIR_ORDER[2 * group + 1])
         n = lax.bitwise_and(jnp.where(leftward, other - pair - 1, pair - 1 - other), PAIRS - 1)
         ring_ref[24 * group : 24 * group + 24, :] = jnp.exp(step * n.astype(F32))
     coefs = [[], [], [], []]
@@ -306,7 +307,7 @@
         product = joined(product, 4 * PEERS, 256)[:, :ROWS]
         added.append(jnp.where(even, product[: 2 * PEERS], product[2 * PEERS :]))
     wall = 2 * lax.axis_index("high") + lax.axis_index("low")
-    mine = 8 * (1 - lax.axis_index("core")) + lax.bitwise_and(wall - FIRST_WALL, WALLS - 1)
+    mine = 8 * (1 - lax.axis_index("core")) + sum(jnp.where(wall == w, i, 0) for i, w in enumerate(WALL_ORDER))
     own_ref[...] = near_ref[pl.ds(pl.multiple_of(8 * mine, 8), 8), :]
     lines = jnp.concatenate(lines, 0) + jnp.concatenate(added, 0)
     lines = jnp.concatenate([lines, jnp.zeros((4 * PEERS, 256 - ROWS), F32)], 1)
@@ -441,13 +442,13 @@
         ],
     )
     near = [2 * core + low for core in (1, 0) for low in range(2)]
-    order = [WALLS * core + (FIRST_WALL + i) % WALLS for core in (1, 0) for i in range(WALLS)]
+    order = [WALLS * core + w for core in (1, 0) for w in WALL_ORDER]
     sent = exchange(sent.reshape(PEERS * CHUNK // 2, 2, COLS), ("core", "high", "low"), order).reshape(PEERS * CHUNK, COLS)
     modes, own, sums = call(
         strip_kernel, [(12 * PAIRS, COLS), (8, COLS), (32, COLS)], [VMEM] * 7,
         sent, chain, reach, pair, rims, mix, into, scratch=[pltpu.VMEM((8 * PEERS, COLS), F32)],
     )
-    modes = exchange(modes.reshape(6 * PAIRS, 2, COLS), "pair", [(FIRST + i) % PAIRS for i in range(PAIRS)]).reshape(12 * PAIRS, COLS)
+    modes = exchange(modes.reshape(6 * PAIRS, 2, COLS), "pair", PAIR_ORDER).reshape(12 * PAIRS, COLS)
     cells = call(
         ring_kernel, [(GROUP * CHUNK, COLS)], [VMEM] * 7, modes, sums, ring, pair, rims, back, cauchy,
         scratch=[pltpu.VMEM((32, COLS), F32)] * 2,

time: 44.8 us -> 44.2 us (0.987)
  blocking collectives: 39.8 us -> 39.1 us
    all_to_all x3, blocking collectives: 39.8 us -> 39.1 us  [exchange(): lax.all_to_all(block, axes, split_axis=0, concat_axis=0, tiled=True, axis...]
where the time goes in v6:
time: 44.2 us; the launch traced here: 43.9 us
  blocking collectives  39.1 us (88%)
  Pallas kernels  4.77 us (11%)
    all_to_all x3, blocking collectives, exchange(): lax.all_to_all(block, axes, split_axis=0, concat_axis=0, tiled=True, axis...  39.1 us
    pallas_call x4, Pallas kernels, call(): pl.pallas_call(kernel, out_shape=outs if len(outs) > 1 else outs[0], in_s...  4.77 us

profile of v6, /device:TPU:1, one launch (start us, length us, event | category | flops | bytes accessed | tf_op | source)
XLA Modules:
  0.0 43.9 jit_solution(6121360129023504120)
XLA Ops:
  0.0 2.4 %shard_map.91 = (f32[160,128]{1,0:T(8,128)S(1)}, f32[384,128]{1,0:T(8,128)S(1)}, f32[384,128]{1,0:T(8,128)S(1)}, bf16[688,256]{1,0:T(8,128)(2,1)S(1)}, f32[512,1...) custom-call(f32[2]{0:T(128)} %wave_hbm.1, ...), custom_call_target="tpu_custom_call" | custom-call | tf_op jit(solution)/shard_map/pallas_call | solution.py:412
  2.4 16.5 %all_to_all.15 = f32[80,2,128]{2,1,0:T(2,128)S(1)} all-to-all(f32[80,2,128]{2,1,0:T(2,128)S(1)} %bitcast.9), channel_id=1, replica_groups={{12,13,11,14,10,15,9,8,4,5,3,6,2,7,1,0},{28,29,27,30,26,31,25,24,20,21,..., dimensions={0} | all-to-all | bytes 163840 | tf_op jit(solution)/shard_map/all_to_all | solution.py:424
  18.9 0.8 %shard_map.92 = (f32[384,128]{1,0:T(8,128)S(1)}, f32[8,128]{1,0:T(8,128)S(1)}, f32[32,128]{1,0:T(8,128)S(1)}) custom-call(f32[160,128]{1,0:T(8,128)S(1)} %bitcast.7, f32[512,128]{1,0:T(8,128)S(1)} %get-tuple-element.22.chain_ref, bf16[256,512]{1,0:T(8,128)(2,1)S(1)} %get-tuple-element.23.reach_ref, f32[80,128]{1,0:T(8,128)S(1)} %get-tuple-element.24.pair_ref, ...), custom_call_target="tpu_custom_call" | custom-call | tf_op jit(solution)/shard_map/pallas_call | solution.py:412
  19.7 15.3 %all_to_all.16 = f32[192,2,128]{2,1,0:T(2,128)S(1)} all-to-all(f32[192,2,128]{2,1,0:T(2,128)S(1)} %bitcast.8), channel_id=1, replica_groups={{368,496,240,112,352,480,224,96,336,464,208,80,320,448,192,64,304,432,1..., dimensions={0} | all-to-all | bytes 393216 | tf_op jit(solution)/shard_map/all_to_all | solution.py:424
  35.0 0.3 shard_map.93
  35.4 7.3 %all_to_all.17 = f32[20,2,128]{2,1,0:T(2,128)S(1)} all-to-all(f32[20,2,128]{2,1,0:T(2,128)S(1)} %bitcast.10), channel_id=1, replica_groups={{8,9,0,1},{10,11,2,3},{12,13,4,5},{14,15,6,7},{24,25,16,17},{26,27,18,1..., dimensions={0} | all-to-all | bytes 40960 | tf_op jit(solution)/shard_map/all_to_all | solution.py:424
  42.6 1.3 %shard_map.94 = f32[2,192,128]{2,1,0:T(8,128)} custom-call(f32[40,128]{1,0:T(8,128)S(1)} %bitcast.11, f32[8,128]{1,0:T(8,128)S(1)} %get-tuple-element.33.own_ref, f32[384,128]{1,0:T(8,128)S(1)} %get-tuple-element.34.freq_ref, f32[384,128]{1,0:T(8,128)S(1)} %get-tuple-element.35.solve_ref, bf16[688,256]{1,0:T(8,128)(2,1)S(1)} %get-tuple-element.36.boxes_ref), custom_call_target="tpu_custom_call" | custom-call | tf_op jit(solution)/shard_map/pallas_call | solution.py:412

commit v7 on v6

--- a/solution.py
+++ b/solution.py
@@ -12,6 +12,7 @@
 NY, NZ = 1536, 8192
 WALLS, STRIPS = 8, 64
 PAIRS, PEERS = STRIPS // 2, 2 * WALLS
+NEAR_ORDER = (3, 2, 1, 0)
 WALL_ORDER = (4, 5, 3, 6, 2, 7, 1, 0)
 PAIR_ORDER = [8 * x + z for z in range(7, -1, -1) for x in (2, 3, 1, 0)]
 ROWS, COLS = NY // WALLS, NZ // STRIPS
@@ -368,11 +369,10 @@
         product = joined(fast(stacked(jnp.concatenate(both, 0)), cauchy_ref[rows, :]), 16)
         rims.append(product[:8] * ends[0:1] + product[8:] * ends[1:2])
     out = []
-    for core in (1, 0):
-        for low in range(2):
-            at = 2 * core + low
-            out += pack([cells[2 * i + core : 2 * i + core + 1, ROWS * low : ROWS * (low + 1)] for i in range(4)])
-            out += [rims[plane][4 * g + at : 4 * g + at + 1] for plane in range(2) for g in range(2)]
+    for at in NEAR_ORDER:
+        core, low = at // 2, at % 2
+        out += pack([cells[2 * i + core : 2 * i + core + 1, ROWS * low : ROWS * (low + 1)] for i in range(4)])
+        out += [rims[plane][4 * g + at : 4 * g + at + 1] for plane in range(2) for g in range(2)]
     out_ref[...] = jnp.concatenate(out, 0)
 
 
@@ -441,7 +441,7 @@
             pltpu.VMEM((SHARED_ROWS, 256), F32), pltpu.VMEM((CLASS_ROWS, COLS), F32), pltpu.SemaphoreType.DMA((10,)),
         ],
     )
-    near = [2 * core + low for core in (1, 0) for low in range(2)]
+    near = list(NEAR_ORDER)
     order = [WALLS * core + w for core in (1, 0) for w in WALL_ORDER]
     sent = exchange(sent.reshape(PEERS * CHUNK // 2, 2, COLS), ("core", "high", "low"), order).reshape(PEERS * CHUNK, COLS)
     modes, own, sums = call(

time: 44.2 us -> 44.1 us (level)
  no operation moved by 1% of the time
where the time goes in v7:
time: 44.1 us; the launch traced here: 43.9 us
  blocking collectives  38.9 us (88%)
  Pallas kernels  4.91 us (11%)
    all_to_all x3, blocking collectives, exchange(): lax.all_to_all(block, axes, split_axis=0, concat_axis=0, tiled=True, axis...  38.9 us
    pallas_call x4, Pallas kernels, call(): pl.pallas_call(kernel, out_shape=outs if len(outs) > 1 else outs[0], in_s...  4.91 us

profile of v7, /device:TPU:1, one launch (start us, length us, event | category | flops | bytes accessed | tf_op | source)
XLA Modules:
  0.0 43.9 jit_solution(3266177592562435473)
XLA Ops:
  0.0 2.4 %shard_map.91 = (f32[160,128]{1,0:T(8,128)S(1)}, f32[384,128]{1,0:T(8,128)S(1)}, f32[384,128]{1,0:T(8,128)S(1)}, bf16[688,256]{1,0:T(8,128)(2,1)S(1)}, f32[512,1...) custom-call(f32[2]{0:T(128)} %wave_hbm.1, ...), custom_call_target="tpu_custom_call" | custom-call | tf_op jit(solution)/shard_map/pallas_call | solution.py:412
  2.4 16.5 %all_to_all.15 = f32[80,2,128]{2,1,0:T(2,128)S(1)} all-to-all(f32[80,2,128]{2,1,0:T(2,128)S(1)} %bitcast.9), channel_id=1, replica_groups={{12,13,11,14,10,15,9,8,4,5,3,6,2,7,1,0},{28,29,27,30,26,31,25,24,20,21,..., dimensions={0} | all-to-all | bytes 163840 | tf_op jit(solution)/shard_map/all_to_all | solution.py:424
  18.9 0.8 %shard_map.92 = (f32[384,128]{1,0:T(8,128)S(1)}, f32[8,128]{1,0:T(8,128)S(1)}, f32[32,128]{1,0:T(8,128)S(1)}) custom-call(f32[160,128]{1,0:T(8,128)S(1)} %bitcast.7, f32[512,128]{1,0:T(8,128)S(1)} %get-tuple-element.22.chain_ref, bf16[256,512]{1,0:T(8,128)(2,1)S(1)} %get-tuple-element.23.reach_ref, f32[80,128]{1,0:T(8,128)S(1)} %get-tuple-element.24.pair_ref, ...), custom_call_target="tpu_custom_call" | custom-call | tf_op jit(solution)/shard_map/pallas_call | solution.py:412
  19.7 15.3 %all_to_all.16 = f32[192,2,128]{2,1,0:T(2,128)S(1)} all-to-all(f32[192,2,128]{2,1,0:T(2,128)S(1)} %bitcast.8), channel_id=1, replica_groups={{368,496,240,112,352,480,224,96,336,464,208,80,320,448,192,64,304,432,1..., dimensions={0} | all-to-all | bytes 393216 | tf_op jit(solution)/shard_map/all_to_all | solution.py:424
  35.0 0.5 %shard_map.93 = f32[40,128]{1,0:T(8,128)S(1)} custom-call(f32[384,128]{1,0:T(8,128)S(1)} %bitcast.6, f32[32,128]{1,0:T(8,128)S(1)} %get-tuple-element.29.sums_ref, f32[384,128]{1,0:T(8,128)S(1)} %get-tuple-element.30.ring_ref, f32[80,128]{1,0:T(8,128)S(1)} %get-tuple-element.24.pair_ref, f32[32,128]{1,0:T(8,128)S(1)} %get-tuple-element.25.rims_ref, ...), custom_call_target="tpu_custom_call" | custom-call | tf_op jit(solution)/shard_map/pallas_call | solution.py:412
  35.5 7.1 %all_to_all.17 = f32[20,2,128]{2,1,0:T(2,128)S(1)} all-to-all(f32[20,2,128]{2,1,0:T(2,128)S(1)} %bitcast.10), channel_id=1, replica_groups={{9,8,1,0},{11,10,3,2},{13,12,5,4},{15,14,7,6},{25,24,17,16},{27,26,19,1..., dimensions={0} | all-to-all | bytes 40960 | tf_op jit(solution)/shard_map/all_to_all | solution.py:424
  42.6 1.3 %shard_map.94 = f32[2,192,128]{2,1,0:T(8,128)} custom-call(f32[40,128]{1,0:T(8,128)S(1)} %bitcast.11, f32[8,128]{1,0:T(8,128)S(1)} %get-tuple-element.33.own_ref, f32[384,128]{1,0:T(8,128)S(1)} %get-tuple-element.34.freq_ref, f32[384,128]{1,0:T(8,128)S(1)} %get-tuple-element.35.solve_ref, bf16[688,256]{1,0:T(8,128)(2,1)S(1)} %get-tuple-element.36.boxes_ref), custom_call_target="tpu_custom_call" | custom-call | tf_op jit(solution)/shard_map/pallas_call | solution.py:412
